TPU v7x, 512 devices: a whole 4x4x16 slice. The times are simulated.
512 devices in a mesh: context: 32 (over y, z_lo, core), tensor: 16 (over x, z_hi).
Axes of the slice: x: 4, y: 4, z: 16 (z_hi: 4, z_lo: 4; z = z_hi * 4 + z_lo), core: 2. Of those that a mesh axis runs over, the one named last changes fastest.
Arguments:
- tokens: bfloat16 [8192, 4096], P(('context', 'tensor')), may hold values from -6 to 6
- x_weight: bfloat16 [4096, 8192], P('context', 'tensor'), may hold values from -0.09375 to 0.09375
- dt_weight: bfloat16 [4096, 128], P('context', 'tensor'), may hold values from -0.09375 to 0.09375
- bc_weight: bfloat16 [8, 4096, 256], P(None, 'context'), may hold values from -0.01953125 to 0.01953125
- conv_x: bfloat16 [4, 8192], P(None, 'tensor'), may hold values from -3 to 3
- conv_bc: bfloat16 [8, 4, 256], replicated, may hold values from -3 to 3
- dt_bias: float32 [128], P('tensor'), may hold values from -1.5 to 0.5
- a_rate: float32 [128], P('tensor'), may hold values from 2.4414063e-05 to 0.08
- d_skip: float32 [128], P('tensor'), may hold values from 0.5 to 1.5
- norm_gain: float32 [8192], P('tensor'), may hold values from 0.1 to 1.9
Outputs:
- normed_out: bfloat16 [8192, 8192], P('context', 'tensor')
All inputs are finite; a program needn't handle non-finite values.
Results may differ from a plain program's by a relative error of at most 0.0085.
Values may be sent and summed in bfloat16 or wider, within the bound.
A program may use at most 64 MiB of HBM per device.

v0:
```python
import jax
import jax.numpy as jnp
from jax import lax
from jax.sharding import PartitionSpec as P

HEADS = 128
HEAD_DIM = 64
STATE = 128
GROUPS = 8
SPAN = 256
CONV = 4


def shifted(block, axis, distance):
    devices = range(lax.axis_size(axis))
    route = [(i - distance, i) for i in devices if i - distance in devices]
    return lax.ppermute(block, axis, route)


def carried_in(part, axis, combine, identity):
    place = lax.axis_index(axis)
    gathered = jax.tree.map(lambda a: lax.all_gather(a, axis), part)
    state = jax.tree.map(lambda a, e: jnp.zeros_like(a) + jnp.asarray(e, a.dtype), part, identity)

    def one(hop, state):
        return combine(
            state, jax.tree.map(lambda a: lax.dynamic_index_in_dim(a, hop, 0, False), gathered)
        )

    return lax.fori_loop(0, place, one, state)


def causal_conv(previous, values, taps):
    count = values.shape[0]
    joined = jnp.concatenate([previous, values], 0).astype(jnp.float32)
    total = jnp.zeros(values.shape, jnp.float32)
    for offset in range(CONV):
        total = total + taps[offset].astype(jnp.float32) * joined[offset : offset + count]
    return jax.nn.silu(total).astype(jnp.bfloat16)


def span_pieces(values, key_query, log_sums, step_sizes):
    length, heads_n, head_width = values.shape
    groups_n = key_query.shape[1]
    per_group = heads_n // groups_n
    inputs_b = key_query[:, :, 0]
    outputs_c = key_query[:, :, 1]
    scores = jnp.einsum("tgn,sgn->gts", outputs_c, inputs_b, preferred_element_type=jnp.float32)
    positions = jnp.arange(length)
    causal_mask = positions[:, None] >= positions[None, :]
    log_gaps = log_sums.T[:, :, None] - log_sums.T[:, None, :]
    decay_table = jnp.where(causal_mask, jnp.exp(jnp.where(causal_mask, log_gaps, 0.0)), 0.0)
    mixing = (
        scores[:, None]
        * decay_table.reshape(groups_n, per_group, length, length)
        * step_sizes.T.reshape(groups_n, per_group, 1, length)
    ).astype(jnp.bfloat16)
    grouped = values.reshape(length, groups_n, per_group, head_width)
    inner_terms = jnp.einsum(
        "gjts,sgjp->tgjp", mixing, grouped, preferred_element_type=jnp.float32
    ).reshape(length, heads_n, head_width)
    tail_weight = jnp.exp(log_sums[-1][None, :] - log_sums) * step_sizes
    weighted = values.astype(jnp.float32) * tail_weight[:, :, None]
    states = jnp.einsum(
        "sgjp,sgn->gjpn",
        weighted.reshape(length, groups_n, per_group, head_width),
        inputs_b.astype(jnp.float32),
        precision=lax.Precision.HIGHEST,
    ).reshape(heads_n, head_width, inputs_b.shape[2])
    return (inner_terms, states)


def span_reads(outputs_c, log_sums, start_state):
    length, groups_n, state_width = outputs_c.shape
    heads_n, head_width = (start_state.shape[0], start_state.shape[1])
    per_group = heads_n // groups_n
    reads = jnp.einsum(
        "tgn,gjpn->tgjp",
        outputs_c.astype(jnp.float32),
        start_state.reshape(groups_n, per_group, head_width, state_width),
        precision=lax.Precision.HIGHEST,
    )
    return reads.reshape(length, heads_n, head_width) * jnp.exp(log_sums)[:, :, None]


def finish(mixed, norm_gain):
    mean_square = jnp.mean(mixed * mixed, axis=-1, keepdims=True)
    normed = (
        mixed * lax.rsqrt(mean_square + 1e-05) * norm_gain.reshape(mixed.shape[1], mixed.shape[2])
    )
    return normed.astype(jnp.bfloat16).reshape(mixed.shape[0], mixed.shape[1] * mixed.shape[2])


def local(
    tokens, x_weight, dt_weight, bc_weight, conv_x, conv_bc, dt_bias, a_rate, d_skip, norm_gain
):
    heads_here = dt_weight.shape[1]
    per_group = HEADS // GROUPS
    groups_here = max(1, heads_here // per_group)
    first_group = lax.axis_index("tensor") * heads_here // per_group
    bc_local = lax.dynamic_slice_in_dim(bc_weight, first_group, groups_here, 0)
    bc_cols = jnp.transpose(bc_local, (1, 0, 2)).reshape(bc_local.shape[1], groups_here * 2 * STATE)
    taps_local = lax.dynamic_slice_in_dim(conv_bc, first_group, groups_here, 0)
    bc_taps = jnp.transpose(taps_local, (1, 0, 2)).reshape(CONV, groups_here * 2 * STATE)
    gathered = lax.all_gather(tokens, "tensor", axis=0, tiled=True)
    pieces = (
        lax.all_gather(x_weight, "context", axis=0, tiled=True),
        lax.all_gather(dt_weight, "context", axis=0, tiled=True),
        lax.all_gather(bc_cols, "context", axis=0, tiled=True),
    )
    x_proj, dt_raw, bc_proj = tuple(
        (jnp.dot(gathered, piece, preferred_element_type=jnp.float32) for piece in pieces)
    )
    rows_here = x_proj.shape[0]
    blocks = rows_here // SPAN
    x_pre = x_proj.astype(jnp.bfloat16)
    bc_pre = bc_proj.astype(jnp.bfloat16)
    rim_x, rim_bc = shifted(
        (x_pre[rows_here - CONV + 1 :], bc_pre[rows_here - CONV + 1 :]), "context", 1
    )
    x_conv = causal_conv(rim_x, x_pre, conv_x)
    bc_conv = causal_conv(rim_bc, bc_pre, bc_taps)
    step_sizes = jax.nn.softplus(dt_raw + dt_bias)
    log_sums = jnp.cumsum((-a_rate * step_sizes).reshape(blocks, SPAN, heads_here), axis=1)
    x_blocks = x_conv.reshape(blocks, SPAN, heads_here, HEAD_DIM)
    bc_blocks = bc_conv.reshape(blocks, SPAN, groups_here, 2, STATE)
    step_blocks = step_sizes.reshape(blocks, SPAN, heads_here)
    inner_terms, block_states = jax.vmap(span_pieces)(x_blocks, bc_blocks, log_sums, step_blocks)
    block_logs = log_sums[:, -1, :]
    carried = jnp.zeros((heads_here, HEAD_DIM, STATE), jnp.float32)
    starts = [carried]
    carried = jnp.exp(block_logs[0])[:, None, None] * carried + block_states[0]
    total_log = jnp.sum(block_logs, 0)

    def combine(earlier, later):
        return (earlier[0] + later[0], jnp.exp(later[0])[:, None, None] * earlier[1] + later[1])

    identity = (jnp.zeros((heads_here,), jnp.float32), jnp.zeros_like(carried))
    _, incoming = carried_in((total_log, carried), "context", combine, identity)
    lead_logs = jnp.cumsum(block_logs, 0) - block_logs
    start_states = jnp.stack(starts) + jnp.exp(lead_logs)[:, :, None, None] * incoming[None]
    reads = jax.vmap(span_reads)(bc_blocks[:, :, :, 1], log_sums, start_states)
    mixed = inner_terms + reads + d_skip[None, None, :, None] * x_blocks.astype(jnp.float32)
    return finish(mixed.reshape(rows_here, heads_here, HEAD_DIM), norm_gain)


def solution(mesh):
    in_specs = (
        P(("context", "tensor"), None),
        P("context", "tensor"),
        P("context", "tensor"),
        P(None, "context", None),
        P(None, "tensor"),
        P(),
        P("tensor"),
        P("tensor"),
        P("tensor"),
        P("tensor"),
    )
    out_specs = P("context", "tensor")
    return jax.shard_map(local, mesh=mesh, in_specs=in_specs, out_specs=out_specs, check_vma=False)
```

profile of v0, /device:TPU:125, one launch (start us, length us, event | category | flops | bytes accessed | tf_op | source)
XLA Modules:
  0.0 368.3 jit_solution(8336581324124974862)
XLA Ops:
  9.7 37.9 %all_gather.23 = bf16[4096,8]{0,1:T(8,128)(2,1)S(1)} all-gather(bf16[128,8]{0,1:T(8,128)(2,1)} %param.14), channel_id=1, replica_groups=mesh['context'=32,'tensor'=16] {'context'}, dimensions={0}, use_global_device_ids=true | all-gather | bytes 67584 | tf_op jit(solution)/shard_map/all_gather | solution.py:108
  48.4 1.4 slice_convert_fusion.3
  49.9 56.7 %all-gather.8.cloned.1.call-done = bf16[256,4096]{1,0:T(8,128)(2,1)} async-done(((bf16[16,4096]{1,0:T(8,128)(2,1)}), bf16[256,4096]{1,0:T(8,128)(2,1)}) %all-gather.8.cloned.1.call-update) | async-done | bytes 2097168 | tf_op jit(solution)/shard_map/all_gather | solution.py:105
  106.6 2.4 compare_select_fusion
  110.8 57.8 %all-gather.12.cloned.1.call-done = bf16[1,4096,256]{2,1,0:T(8,128)(2,1)} async-done(((bf16[1,128,256]{2,1,0:T(8,128)(2,1)}), bf16[1,4096,256]{2,1,0:T(8,128)(2,1)}) %all-gather.12.cloned.1.call-update) | async-done | bytes 2097168 | tf_op jit(solution)/shard_map/all_gather | solution.py:109
  168.6 2.3 fusion.5
  170.9 1.3 collective-permute-start.1
  174.2 63.7 %all-gather.10.cloned.1.call-done = bf16[4096,512]{1,0:T(8,128)(2,1)} async-done(((bf16[128,512]{1,0:T(8,128)(2,1)}), bf16[4096,512]{1,0:T(8,128)(2,1)}) %all-gather.10.cloned.1.call-update) | async-done | bytes 4194320 | tf_op jit(solution)/shard_map/all_gather | solution.py:107
  237.9 3.4 convolution_convert_fusion
  241.3 1.3 collective-permute-start
  242.8 1.6 collective-permute-done
  245.2 1.1 convolution_add_fusion
  247.4 38.6 %all-gather.1 = f32[32,1,8]{2,1,0:T(1,128)S(1)} all-gather(f32[1,1,8]{2,1,0:T(1,128)S(1)} %copy.34), channel_id=3, replica_groups=mesh['context'=32,'tensor'=16] {'context'}, dimensions={0}, use_global_device_ids=true | all-gather | bytes 1056 | tf_op jit(solution)/shard_map/all_gather | solution.py:22
  287.5 37.1 %all-gather.14.cloned.1.call-done = f32[256,64,128]{2,1,0:T(8,128)} async-done(((f32[8,64,128]{2,1,0:T(8,128)}), f32[256,64,128]{2,1,0:T(8,128)}) %all-gather.14.cloned.1.call-update) | async-done | bytes 8388624 | tf_op jit(solution)/shard_map/all_gather | solution.py:22
  324.6 34.4 %while.12 = (s32[]{:T(128)}, f32[8,64,128]{2,1,0:T(8,128)S(1)}, s32[]{:T(128)}, f32[32,8]{1,0:T(8,128)S(1)}, f32[32,8,64,128]{3,2,1,0:T(8,128)}, /*index=5*/s32[]{:T(128)}, s32[]{:T(128)}, s32[]{:T(128)}) while((s32[]{:T(128)}, f32[8,64,128]{2,1,0:T(8,128)S(1)}, s32[]{:T(128)}, f32[32,8]{1,0:T(8,128)S(1)}, f32[32,8,64,128]{3,2,1,0:T(8,128)}, ...), condition=%wide.region_3.4_spmd, body=%wide.region_2.3_spmd.sunk | while | flops 131077 | bytes 786655 | solution.py:30
  324.6 1.1 bitcast_add_fusion.4
  326.9 1.1 bitcast_add_fusion.4
  329.1 1.1 bitcast_add_fusion.4
  330.2 1.1 bitcast_add_fusion.4
  332.4 1.1 bitcast_add_fusion.4
  333.5 1.1 bitcast_add_fusion.4
  335.7 1.1 bitcast_add_fusion.4
  337.9 1.1 bitcast_add_fusion.4
  339.0 1.1 bitcast_add_fusion.4
  341.3 1.1 bitcast_add_fusion.4
  342.4 1.1 bitcast_add_fusion.4
  344.6 1.1 bitcast_add_fusion.4
  345.7 1.1 bitcast_add_fusion.4
  347.9 1.1 bitcast_add_fusion.4
  350.1 1.1 bitcast_add_fusion.4
  351.2 1.1 bitcast_add_fusion.4
  359.0 1.1 fusion.25
  (127 shorter events, 29.0 us)
Async XLA Ops:
  6.5 1.0 copy-start
  6.5 100.0 %all-gather.8.cloned.1.call-start = ((), (), s32[]{:S(2)}) async-start(), calls=%async_computation | async-start | bytes 2228224 | tf_op jit(solution)/shard_map/all_gather | solution.py:105
  7.3 161.3 %all-gather.12.cloned.1.call-start = ((), (), s32[]{:S(2)}) async-start(), calls=%async_computation.2 | async-start | bytes 2162688 | tf_op jit(solution)/shard_map/all_gather | solution.py:109
  8.2 229.6 %all-gather.10.cloned.1.call-start = ((), (), s32[]{:S(2)}) async-start(), calls=%async_computation.1 | async-start | bytes 4325376 | tf_op jit(solution)/shard_map/all_gather | solution.py:107
  9.0 315.6 %all-gather.14.cloned.1.call-start = ((), (), s32[]{:S(2)}) async-start(), calls=%async_computation.3 | async-start | bytes 8650752 | tf_op jit(solution)/shard_map/all_gather | solution.py:22
  106.6 62.0 %copy-start.1 = (bf16[256,4096]{1,0:T(8,128)(2,1)S(1)}, bf16[256,4096]{1,0:T(8,128)(2,1)}, u32[]{:S(2)}) copy-start(bf16[256,4096]{1,0:T(8,128)(2,1)} %all-gather.8.cloned.1.call-done) | copy-start | bytes 6291460
  109.0 61.9 %copy-start.3 = (f32[256,8]{0,1:T(8,128)}, f32[256,8]{0,1:T(8,128)S(1)}, u32[]{:S(2)}) copy-start(f32[256,8]{0,1:T(8,128)S(1)} %compare_select_fusion) | copy-start | bytes 24580
  109.8 61.0 %copy-start.6 = (f32[8,2]{0,1:T(2,128)}, f32[8,2]{0,1:T(2,128)S(1)}, u32[]{:S(2)}) copy-start(f32[8,2]{0,1:T(2,128)S(1)} %slice_bitcast_fusion) | copy-start | bytes 196
  170.9 3.1 collective-permute-start.1
  174.2 70.3 %copy-start.2 = (f32[256,512]{1,0:T(8,128)S(1)}, f32[256,512]{1,0:T(8,128)}, u32[]{:S(2)}) copy-start(f32[256,512]{1,0:T(8,128)} %copy.36) | copy-start | bytes 1572868
  237.9 6.6 %copy-start.9 = (f32[1,512]{1,0:T(1,128)S(1)}, f32[1,512]{1,0:T(1,128)}, u32[]{:S(2)}) copy-start(f32[1,512]{1,0:T(1,128)} %get-tuple-element.82) | copy-start | bytes 6148
  237.9 6.6 %copy-start.10 = (f32[1,512]{1,0:T(1,128)S(1)}, f32[1,512]{1,0:T(1,128)}, u32[]{:S(2)}) copy-start(f32[1,512]{1,0:T(1,128)} %get-tuple-element.83) | copy-start | bytes 6148
  237.9 6.6 %copy-start.11 = (f32[1,512]{1,0:T(1,128)S(1)}, f32[1,512]{1,0:T(1,128)}, u32[]{:S(2)}) copy-start(f32[1,512]{1,0:T(1,128)} %get-tuple-element.84) | copy-start | bytes 6148
  237.9 6.6 %copy-start.12 = (f32[1,512]{1,0:T(1,128)S(1)}, f32[1,512]{1,0:T(1,128)}, u32[]{:S(2)}) copy-start(f32[1,512]{1,0:T(1,128)} %get-tuple-element.85) | copy-start | bytes 6148
  241.3 3.1 collective-permute-start
  244.5 0.7 copy-start.15
  244.5 1.8 copy-start.14
  244.5 2.5 copy-start.5
  244.9 41.1 %copy-start.7 = (f32[8,2]{0,1:T(2,128)S(1)}, f32[8,2]{0,1:T(2,128)}, u32[]{:S(2)}) copy-start(f32[8,2]{0,1:T(2,128)} %copy-done.6) | copy-start | bytes 196
  245.1 41.3 %copy-start.4 = (f32[256,8]{0,1:T(8,128)S(1)}, f32[256,8]{0,1:T(8,128)}, u32[]{:S(2)}) copy-start(f32[256,8]{0,1:T(8,128)} %copy-done.3) | copy-start | bytes 24580
  360.1 0.7 copy-start.8
  360.1 0.7 copy-start.13
Sparse Core Ops, SparseCore 0:
  10.4 96.1 all-gather.7
  108.7 59.8 all-gather.11
  170.7 67.1 all-gather.9
  246.4 78.1 all-gather.13
where the time goes:
time: 370 us; the launch traced here: 368 us
  waiting for transfers between devices  218 us (59%)
  blocking collectives  76.6 us (21%)
  other arithmetic  38.9 us (11%)
  between operations  13.5 us (4%)
  matrix products  11.3 us (3%)
  local copies, waits for them, and re-layouts  5.83 us (2%)
    all_gather x1, waiting for transfers between devices, local(): lax.all_gather(x_weight, 'context', axis=0, tiled=True)  63.7 us
    all_gather x1, waiting for transfers between devices, local(): lax.all_gather(bc_cols, 'context', axis=0, tiled=True)  57.8 us
    all_gather x1, waiting for transfers between devices, local(): gathered = lax.all_gather(tokens, 'tensor', axis=0, tiled=True)  56.7 us
    all_gather x1, blocking collectives, carried_in(): gathered = jax.tree.map(lambda a: lax.all_gather(a, axis), part)  38.6 us
    all_gather x1, blocking collectives, local(): lax.all_gather(dt_weight, 'context', axis=0, tiled=True)  37.9 us
    all_gather x1, waiting for transfers between devices, carried_in(): gathered = jax.tree.map(lambda a: lax.all_gather(a, axis), part)  37.1 us
    add x31, other arithmetic, combine(): jnp.exp(later[0])[:, None, None] * earlier[1] + later[1]  32.9 us
    dot_general x3, matrix products, local(): jnp.dot(gathered, piece, preferred_element_type=jnp.float32)  8.13 us
  transfers between devices with their start and end apart: 6, of which 6 were waited for; matrix products, arithmetic and copies ran while one was open for 4% of the time, Pallas kernels for 0%

commit v1 on v0

--- a/solution.py
+++ b/solution.py
@@ -1,7 +1,13 @@
+import functools
+
 import jax
 import jax.numpy as jnp
 from jax import lax
+from jax.experimental import pallas as pl
+from jax.experimental.pallas import tpu as pltpu
 from jax.sharding import PartitionSpec as P
+
+MESH = pl.DeviceIdType.MESH
 
 HEADS = 128
 HEAD_DIM = 64
@@ -9,6 +15,212 @@
 GROUPS = 8
 SPAN = 256
 CONV = 4
+
+
+def place():
+    c = lax.axis_index("context")
+    t = lax.axis_index("tensor")
+    return t // 4, c // 8, t % 4, (c // 2) % 4, c % 2
+
+
+def device(x, y, z_hi, z_lo, core):
+    return ((y % 4) * 8 + (z_lo % 4) * 2 + core, (x % 4) * 4 + z_hi % 4)
+
+
+def along_z(z, by):
+    other = (z + by + 16) % 16
+    return other // 4, other % 4
+
+
+def project_kernel(
+    tok_ref, w_ref, dt_ref, bc_ref,
+    x_out, bc_out, dt_out,
+    tok, wb, dts,
+    local_sem, tz_s, tz_r, tx_s, tx_r, wz_s, wz_r, bz_s, bz_r,
+    wy_s, wy_r, wc_s, wc_r, dz_s, dz_r, dy_s, dy_r, dc_s, dc_r,
+):
+    x, y, z_hi, z_lo, core = place()
+    z = z_hi * 4 + z_lo
+    t_own = x * 4 + z_hi
+    sibling = device(x, y, z_hi, z_lo, 1 - core)
+
+    def send(src, dst, ssem, rsem, dev):
+        copy = pltpu.make_async_remote_copy(
+            src_ref=src, dst_ref=dst, send_sem=ssem, recv_sem=rsem, device_id=dev, device_id_type=MESH
+        )
+        copy.start()
+        return copy
+
+    def piece(y_at, z_at, core_at):
+        return (y_at % 4) * 8 + (z_at % 4) * 2 + core_at
+
+    own = piece(y, z_lo, core)
+    group = x * 2 + z_hi // 2
+    local = [
+        pltpu.make_async_copy(tok_ref, tok.at[t_own], local_sem.at[0]),
+        pltpu.make_async_copy(w_ref, wb.at[own, :, pl.ds(0, 512)], local_sem.at[1]),
+        pltpu.make_async_copy(bc_ref.at[group], wb.at[own, :, pl.ds(512, 256)], local_sem.at[2]),
+    ]
+    for copy in local:
+        copy.start()
+    square = jnp.concatenate([dt_ref[...].astype(jnp.float32), jnp.zeros((128, 120), jnp.float32)], 1)
+    dts[core, y, z_lo] = square.T[:16].astype(jnp.bfloat16)
+
+    barrier = pltpu.get_barrier_semaphore()
+    partners = [device(x, y, z_hi + 1, z_lo, core), device(x, y, z_hi + 3, z_lo, core), sibling]
+    for by in (1, 2, 3):
+        partners.append(device(x + by, y, z_hi, z_lo, core))
+        partners.append(device(x, y + by, z_hi, z_lo, core))
+        partners.append(device(x, y, z_hi, z_lo + by, core))
+    for by in (1, -1, 2, -2):
+        partners.append(device(x, y, *along_z(z, by), core))
+    for partner in partners:
+        pl.semaphore_signal(barrier, inc=1, device_id=partner, device_id_type=MESH)
+    pl.semaphore_wait(barrier, len(partners))
+
+    started = []
+    dz = [
+        send(dts.at[core, y, z_lo], dts.at[core, y, z_lo], dz_s.at[by], dz_r.at[by], device(x, y, z_hi, z_lo + by, core))
+        for by in (1, 2, 3)
+    ]
+    wz = [
+        send(w_ref, wb.at[own, :, pl.ds(0, 512)], wz_s.at[by], wz_r.at[by], device(x, y, z_hi, z_lo + by, core))
+        for by in (1, 2, 3)
+    ]
+    bz = []
+    for i, (by, first, count) in enumerate(((1, 0, 128), (-1, 0, 128), (2, 0, 64), (-2, 64, 64))):
+        hi, lo = along_z(z, by)
+        bz.append(
+            send(
+                bc_ref.at[x * 2 + hi // 2, pl.ds(first, count)],
+                wb.at[own, pl.ds(first, count), pl.ds(512, 256)],
+                bz_s.at[i], bz_r.at[i], device(x, y, hi, lo, core),
+            )
+        )
+    tz = [
+        send(tok_ref, tok.at[t_own], tz_s.at[0], tz_r.at[0], device(x, y, z_hi + 1, z_lo, core)),
+        send(tok_ref, tok.at[t_own], tz_s.at[1], tz_r.at[1], device(x, y, z_hi + 3, z_lo, core)),
+    ]
+    for copy in local:
+        copy.wait()
+
+    tx = []
+
+    def tokens_along_x(k, hi):
+        slot = tok.at[x * 4 + hi]
+        for by in (1, 2, 3):
+            tx.append(
+                send(slot, slot, tx_s.at[k, by], tx_r.at[k, by], device(x + by, y, z_hi, z_lo, core))
+            )
+
+    wy = {}
+
+    def rows_along_y(k):
+        slot = wb.at[piece(y, z_lo + k, core)]
+        wy[k, 0] = send(slot, slot, wy_s.at[k, 0], wy_r.at[k, 0], device(x, y + 1, z_hi, z_lo, core))
+        wy[k, 1] = send(slot, slot, wy_s.at[k, 1], wy_r.at[k, 1], device(x, y + 3, z_hi, z_lo, core))
+
+    def relay_along_y(k):
+        wy[k, 0].wait_recv()
+        half = wb.at[piece(y + 3, z_lo + k, core), pl.ds(0, 64)]
+        wy[k, 2] = send(half, half, wy_s.at[k, 2], wy_r.at[k, 2], device(x, y + 1, z_hi, z_lo, core))
+        wy[k, 1].wait_recv()
+        half = wb.at[piece(y + 1, z_lo + k, core), pl.ds(64, 64)]
+        wy[k, 3] = send(half, half, wy_s.at[k, 3], wy_r.at[k, 3], device(x, y + 3, z_hi, z_lo, core))
+        to_sibling(k, 3)
+        to_sibling(k, 1)
+
+    wc = []
+
+    def to_sibling(k, by):
+        slot = wb.at[piece(y + by, z_lo + k, core)]
+        wc.append(send(slot, slot, wc_s.at[k, by], wc_r.at[k, by], sibling))
+
+    rows_along_y(0)
+    tokens_along_x(0, z_hi)
+    to_sibling(0, 0)
+
+    for copy in dz:
+        copy.wait_recv()
+    block = dts.at[core, y]
+    dy = [
+        send(block, block, dy_s.at[by], dy_r.at[by], device(x, y + by, z_hi, z_lo, core)) for by in (1, 2, 3)
+    ]
+
+    for copy in bz:
+        copy.wait_recv()
+    for by in (1, 3, 2):
+        wz[by - 1].wait_recv()
+        rows_along_y(4 - by)
+        to_sibling(4 - by, 0)
+    relay_along_y(0)
+    for copy in dy:
+        copy.wait_recv()
+    block = dts.at[core]
+    dc = send(block, block, dc_s, dc_r, sibling)
+
+    tz[0].wait_recv()
+    half = tok.at[x * 4 + (z_hi + 3) % 4, :, pl.ds(0, 2048)]
+    tz.append(send(half, half, tz_s.at[2], tz_r.at[2], device(x, y, z_hi + 1, z_lo, core)))
+    tz[1].wait_recv()
+    half = tok.at[x * 4 + (z_hi + 1) % 4, :, pl.ds(2048, 2048)]
+    tz.append(send(half, half, tz_s.at[3], tz_r.at[3], device(x, y, z_hi + 3, z_lo, core)))
+    tokens_along_x(1, (z_hi + 3) % 4)
+    tokens_along_x(2, (z_hi + 1) % 4)
+
+    for k in (3, 1, 2):
+        relay_along_y(k)
+    tz[2].wait_recv()
+    tz[3].wait_recv()
+    tokens_along_x(3, (z_hi + 2) % 4)
+    for k in (0, 3, 1, 2):
+        wy[k, 2].wait_recv()
+        wy[k, 3].wait_recv()
+        to_sibling(k, 2)
+    for copy in tx:
+        copy.wait_recv()
+    dc.wait_recv()
+    for copy in wc:
+        copy.wait_recv()
+
+    rows = tok[...].reshape(256, 4096)
+    dt_cols = jnp.concatenate([dts[p % 2, p // 8, (p // 2) % 4] for p in range(32)], 1)
+    dt_out[...] = lax.dot_general(rows, dt_cols, (((1,), (1,)), ((), ())), preferred_element_type=jnp.float32)
+    both = jnp.dot(rows, wb[...].reshape(4096, 768), preferred_element_type=jnp.float32)
+    x_out[...] = both[:, :512].astype(jnp.bfloat16)
+    bc_out[...] = both[:, 512:].astype(jnp.bfloat16)
+
+    for copy in dz + wz + bz + tz + tx + list(wy.values()) + wc + dy + [dc]:
+        copy.wait_send()
+
+
+def project(tokens, x_weight, dt_weight, bc_weight):
+    dma = pltpu.SemaphoreType.DMA
+    return pl.pallas_call(
+        project_kernel,
+        out_shape=(
+            jax.ShapeDtypeStruct((256, 512), jnp.bfloat16),
+            jax.ShapeDtypeStruct((256, 256), jnp.bfloat16),
+            jax.ShapeDtypeStruct((256, 16), jnp.float32),
+        ),
+        in_specs=[
+            pl.BlockSpec(memory_space=pl.ANY),
+            pl.BlockSpec(memory_space=pl.ANY),
+            pl.BlockSpec(memory_space=pltpu.VMEM),
+            pl.BlockSpec(memory_space=pl.ANY),
+        ],
+        out_specs=[pl.BlockSpec(memory_space=pltpu.VMEM)] * 3,
+        scratch_shapes=[
+            pltpu.VMEM((16, 16, 4096), jnp.bfloat16),
+            pltpu.VMEM((32, 128, 768), jnp.bfloat16),
+            pltpu.VMEM((2, 4, 4, 16, 128), jnp.bfloat16),
+            dma((3,)),
+            dma((4,)), dma((4,)), dma((4, 4)), dma((4, 4)), dma((4,)), dma((4,)), dma((4,)), dma((4,)),
+            dma((4, 4)), dma((4, 4)), dma((4, 4)), dma((4, 4)), dma((4,)), dma((4,)), dma((4,)), dma((4,)), dma, dma,
+        ],
+        compiler_params=pltpu.CompilerParams(collective_id=0, has_side_effects=True, vmem_limit_bytes=50 * 2**20),
+        name="project",
+    )(tokens, x_weight, dt_weight, bc_weight)
 
 
 def shifted(block, axis, distance):
@@ -98,23 +310,12 @@
     per_group = HEADS // GROUPS
     groups_here = max(1, heads_here // per_group)
     first_group = lax.axis_index("tensor") * heads_here // per_group
-    bc_local = lax.dynamic_slice_in_dim(bc_weight, first_group, groups_here, 0)
-    bc_cols = jnp.transpose(bc_local, (1, 0, 2)).reshape(bc_local.shape[1], groups_here * 2 * STATE)
     taps_local = lax.dynamic_slice_in_dim(conv_bc, first_group, groups_here, 0)
     bc_taps = jnp.transpose(taps_local, (1, 0, 2)).reshape(CONV, groups_here * 2 * STATE)
-    gathered = lax.all_gather(tokens, "tensor", axis=0, tiled=True)
-    pieces = (
-        lax.all_gather(x_weight, "context", axis=0, tiled=True),
-        lax.all_gather(dt_weight, "context", axis=0, tiled=True),
-        lax.all_gather(bc_cols, "context", axis=0, tiled=True),
-    )
-    x_proj, dt_raw, bc_proj = tuple(
-        (jnp.dot(gathered, piece, preferred_element_type=jnp.float32) for piece in pieces)
-    )
-    rows_here = x_proj.shape[0]
+    x_pre, bc_pre, dt_wide = project(tokens, x_weight, dt_weight, bc_weight)
+    dt_raw = dt_wide[:, :heads_here]
+    rows_here = x_pre.shape[0]
     blocks = rows_here // SPAN
-    x_pre = x_proj.astype(jnp.bfloat16)
-    bc_pre = bc_proj.astype(jnp.bfloat16)
     rim_x, rim_bc = shifted(
         (x_pre[rows_here - CONV + 1 :], bc_pre[rows_here - CONV + 1 :]), "context", 1
     )

time: 370 us -> 198 us (0.54)
  the two profiles are of different devices: /device:TPU:125 before, /device:TPU:123 now
where the time goes in v1:
time: 198 us; the launch traced here: 197 us
  Pallas kernels  60.8 us (31%)
  blocking collectives  39.1 us (20%)
  other arithmetic  39 us (20%)
  waiting for transfers between devices  31.8 us (16%)
  between operations  13.7 us (7%)
  local copies, waits for them, and re-layouts  6.57 us (3%)
  starting transfers between devices  2.59 us (1%)
  matrix products  2.54 us (1%)
    pallas_call x1, Pallas kernels, project(): pl.pallas_call(project_kernel, out_shape=(jax.ShapeDtypeStruct((256, 512)...  60.8 us
    all_gather x1, blocking collectives, carried_in(): gathered = jax.tree.map(lambda a: lax.all_gather(a, axis), part)  39.1 us
    add x31, other arithmetic, combine(): jnp.exp(later[0])[:, None, None] * earlier[1] + later[1]  32.9 us
    all_gather x1, waiting for transfers between devices, carried_in(): gathered = jax.tree.map(lambda a: lax.all_gather(a, axis), part)  31.8 us
  transfers between devices with their start and end apart: 3, of which 1 were waited for; matrix products, arithmetic and copies ran while one was open for 4% of the time, Pallas kernels for 0%

profile of v1, /device:TPU:123, one launch (start us, length us, event | category | flops | bytes accessed | tf_op | source)
XLA Modules:
  0.0 197.2 jit_solution(568860293127541319)
XLA Ops:
  10.2 60.8 %project.1 = (bf16[256,512]{1,0:T(8,128)(2,1)S(1)}, bf16[256,256]{1,0:T(8,128)(2,1)S(1)}, f32[256,16]{1,0:T(8,128)S(1)}) custom-call(bf16[16,4096]{1,0:T(8,128)(2,1)S(1)} %copy-done.1, bf16[128,512]{1,0:T(8,128)(2,1)S(1)} %copy-done.2, bf16[128,8]{1,0:T(8,128)(2,1)S(1)} %copy.57.dt_ref, bf16[8,128,256]{2,1,0:T(8,128)(2,1)S(1)} %copy-done), custom_call_target="tpu_custom_call" | custom-call | tf_op jit(solution)/shard_map/project/pallas_call | solution.py:199
  71.0 1.3 collective-permute-start.1
  72.3 1.3 collective-permute-start
  80.0 1.1 convolution_add_fusion
  81.7 39.1 %all-gather = f32[32,1,8]{2,1,0:T(1,128)S(1)} all-gather(f32[1,1,8]{2,1,0:T(1,128)S(1)} %get-tuple-element.77), channel_id=2, replica_groups=mesh['context'=32,'tensor'=16] {'context'}, dimensions={0}, use_global_device_ids=true | all-gather | bytes 1056 | tf_op jit(solution)/shard_map/all_gather | solution.py:234
  122.2 31.8 %all-gather.4.cloned.1.call-done = f32[256,64,128]{2,1,0:T(8,128)} async-done(((f32[8,64,128]{2,1,0:T(8,128)}), f32[256,64,128]{2,1,0:T(8,128)}) %all-gather.4.cloned.1.call-update) | async-done | bytes 8388624 | tf_op jit(solution)/shard_map/all_gather | solution.py:234
  154.1 34.3 %while.12 = (s32[]{:T(128)}, f32[8,64,128]{2,1,0:T(8,128)S(1)}, s32[]{:T(128)}, f32[32,8]{1,0:T(8,128)S(1)}, f32[32,8,64,128]{3,2,1,0:T(8,128)}, /*index=5*/s32[]{:T(128)}, s32[]{:T(128)}, s32[]{:T(128)}) while((s32[]{:T(128)}, f32[8,64,128]{2,1,0:T(8,128)S(1)}, s32[]{:T(128)}, f32[32,8]{1,0:T(8,128)S(1)}, f32[32,8,64,128]{3,2,1,0:T(8,128)}, ...), condition=%wide.region_3.4_spmd, body=%wide.region_2.3_spmd.sunk | while | flops 131077 | bytes 786663 | solution.py:242
  154.1 1.1 bitcast_add_fusion.5
  155.2 1.1 bitcast_add_fusion.5
  156.3 1.1 bitcast_add_fusion.5
  157.4 1.1 bitcast_add_fusion.5
  158.5 1.1 bitcast_add_fusion.5
  159.6 1.1 bitcast_add_fusion.5
  160.8 1.1 bitcast_add_fusion.5
  161.9 1.1 bitcast_add_fusion.5
  163.0 1.1 bitcast_add_fusion.5
  164.1 1.1 bitcast_add_fusion.5
  165.2 1.1 bitcast_add_fusion.5
  166.3 1.1 bitcast_add_fusion.5
  167.4 1.1 bitcast_add_fusion.5
  169.6 1.1 bitcast_add_fusion.5
  170.7 1.1 bitcast_add_fusion.5
  171.8 1.1 bitcast_add_fusion.5
  175.1 1.1 bitcast_add_fusion.5
  176.2 1.1 bitcast_add_fusion.5
  177.3 1.1 bitcast_add_fusion.5
  180.7 1.1 bitcast_add_fusion.5
  181.8 1.1 bitcast_add_fusion.5
  182.9 1.1 bitcast_add_fusion.5
  185.1 1.1 bitcast_add_fusion.5
  186.2 1.1 bitcast_add_fusion.5
  187.3 1.1 bitcast_add_fusion.5
  (99 shorter events, 20.6 us)
Async XLA Ops:
  6.5 147.5 %all-gather.4.cloned.1.call-start = ((), (), s32[]{:S(2)}) async-start(), calls=%async_computation | async-start | bytes 8650752 | tf_op jit(solution)/shard_map/all_gather | solution.py:234
  7.3 1.0 copy-start
  8.4 0.9 copy-start.1
  9.3 0.9 copy-start.2
  71.0 7.9 %collective-permute-start.1 = (bf16[3,256]{1,0:T(4,128)(2,1)S(1)}, bf16[3,256]{1,0:T(4,128)(2,1)S(1)}, u32[]{:S(2)}, u32[]{:S(2)}) collective-permute-start(bf16[3,256]{1,0:T(4,128)(2,1)S(1)} %slice.88), channel_id=1, source_target_pairs={{0,16},{16,32},{32,48},{48,64},{64,80},{80,96},{96,112},{112,128},... | collective-permute-start | bytes 4616 | tf_op jit(solution)/shard_map/ppermute | solution.py:229
  72.3 7.0 %collective-permute-start = (bf16[3,512]{1,0:T(4,128)(2,1)S(1)}, bf16[3,512]{1,0:T(4,128)(2,1)S(1)}, u32[]{:S(2)}, u32[]{:S(2)}) collective-permute-start(bf16[3,512]{1,0:T(4,128)(2,1)S(1)} %slice.79), channel_id=1, source_target_pairs={{0,16},{16,32},{32,48},{48,64},{64,80},{80,96},{96,112},{112,128},... | collective-permute-start | bytes 9224 | tf_op jit(solution)/shard_map/ppermute | solution.py:229
  79.4 1.7 copy-start.4
  188.4 1.0 copy-start.3
Sparse Core Ops, SparseCore 0:
  81.2 72.7 all-gather.3

commit v2 on v1

v2 whole, which is shorter than its diff:
```python
import jax
import jax.numpy as jnp
from jax import lax
from jax.experimental import pallas as pl
from jax.experimental.pallas import tpu as pltpu
from jax.sharding import PartitionSpec as P

MESH = pl.DeviceIdType.MESH

HEAD_DIM = 64
STATE = 128
SPAN = 256
CONV = 4
CONTEXTS = 32


def place():
    c = lax.axis_index("context")
    t = lax.axis_index("tensor")
    return t // 4, c // 8, t % 4, (c // 2) % 4, c % 2


def device(x, y, z_hi, z_lo, core):
    return ((y % 4) * 8 + (z_lo % 4) * 2 + core, (x % 4) * 4 + z_hi % 4)


def along_z(z, by):
    other = (z + by + 16) % 16
    return other // 4, other % 4


def layer_kernel(
    tok_ref, w_ref, dt_ref, bc_ref, conv_x_ref, conv_bc_ref, bias_ref, rate_ref, skip_ref, gain_ref,
    out_ref,
    tok, wb, dts, pre, inner, decays, mine, theirs, leaving, arriving,
    local_sem, tz_s, tz_r, tx_s, tx_r, wz_s, wz_r, bz_s, bz_r,
    wy_s, wy_r, wc_s, wc_r, dz_s, dz_r, dy_s, dy_r, dc_s, dc_r,
    rim_s, rim_r, decay_s, decay_r, state_s, state_r, start_s, start_r,
):
    x, y, z_hi, z_lo, core = place()
    z = z_hi * 4 + z_lo
    t_own = x * 4 + z_hi
    sibling = device(x, y, z_hi, z_lo, 1 - core)

    def send(src, dst, ssem, rsem, dev):
        copy = pltpu.make_async_remote_copy(
            src_ref=src, dst_ref=dst, send_sem=ssem, recv_sem=rsem, device_id=dev, device_id_type=MESH
        )
        copy.start()
        return copy

    def piece(y_at, z_at, core_at):
        return (y_at % 4) * 8 + (z_at % 4) * 2 + core_at

    own = piece(y, z_lo, core)
    group = x * 2 + z_hi // 2
    local = [
        pltpu.make_async_copy(tok_ref, tok.at[t_own], local_sem.at[0]),
        pltpu.make_async_copy(w_ref, wb.at[own, :, pl.ds(0, 512)], local_sem.at[1]),
        pltpu.make_async_copy(bc_ref.at[group], wb.at[own, :, pl.ds(512, 256)], local_sem.at[2]),
    ]
    for copy in local:
        copy.start()
    square = jnp.concatenate([dt_ref[...].astype(jnp.float32), jnp.zeros((128, 120), jnp.float32)], 1)
    dts[core, y, z_lo] = square.T[:16].astype(jnp.bfloat16)

    barrier = pltpu.get_barrier_semaphore()
    partners = [device(x, y, z_hi + 1, z_lo, core), device(x, y, z_hi + 3, z_lo, core), sibling]
    for by in (1, 2, 3):
        partners.append(device(x + by, y, z_hi, z_lo, core))
        partners.append(device(x, y + by, z_hi, z_lo, core))
        partners.append(device(x, y, z_hi, z_lo + by, core))
    for by in (1, -1, 2, -2):
        partners.append(device(x, y, *along_z(z, by), core))
    c = lax.axis_index("context")
    for by in (1, CONTEXTS - 1):
        partners.append(((c + by) % CONTEXTS, t_own))
    for partner in partners:
        pl.semaphore_signal(barrier, inc=1, device_id=partner, device_id_type=MESH)
    pl.semaphore_wait(barrier, len(partners))

    started = []
    dz = [
        send(dts.at[core, y, z_lo], dts.at[core, y, z_lo], dz_s.at[by], dz_r.at[by], device(x, y, z_hi, z_lo + by, core))
        for by in (1, 2, 3)
    ]
    wz = [
        send(w_ref, wb.at[own, :, pl.ds(0, 512)], wz_s.at[by], wz_r.at[by], device(x, y, z_hi, z_lo + by, core))
        for by in (1, 2, 3)
    ]
    bz = []
    for i, (by, first, count) in enumerate(((1, 0, 128), (-1, 0, 128), (2, 0, 64), (-2, 64, 64))):
        hi, lo = along_z(z, by)
        bz.append(
            send(
                bc_ref.at[x * 2 + hi // 2, pl.ds(first, count)],
                wb.at[own, pl.ds(first, count), pl.ds(512, 256)],
                bz_s.at[i], bz_r.at[i], device(x, y, hi, lo, core),
            )
        )
    tz = [
        send(tok_ref, tok.at[t_own], tz_s.at[0], tz_r.at[0], device(x, y, z_hi + 1, z_lo, core)),
        send(tok_ref, tok.at[t_own], tz_s.at[1], tz_r.at[1], device(x, y, z_hi + 3, z_lo, core)),
    ]
    for copy in local:
        copy.wait()

    tx = []

    def tokens_along_x(k, hi):
        slot = tok.at[x * 4 + hi]
        for by in (1, 2, 3):
            tx.append(
                send(slot, slot, tx_s.at[k, by], tx_r.at[k, by], device(x + by, y, z_hi, z_lo, core))
            )

    wy = {}

    def rows_along_y(k):
        slot = wb.at[piece(y, z_lo + k, core)]
        wy[k, 0] = send(slot, slot, wy_s.at[k, 0], wy_r.at[k, 0], device(x, y + 1, z_hi, z_lo, core))
        wy[k, 1] = send(slot, slot, wy_s.at[k, 1], wy_r.at[k, 1], device(x, y + 3, z_hi, z_lo, core))

    def relay_along_y(k):
        wy[k, 0].wait_recv()
        half = wb.at[piece(y + 3, z_lo + k, core), pl.ds(0, 64)]
        wy[k, 2] = send(half, half, wy_s.at[k, 2], wy_r.at[k, 2], device(x, y + 1, z_hi, z_lo, core))
        wy[k, 1].wait_recv()
        half = wb.at[piece(y + 1, z_lo + k, core), pl.ds(64, 64)]
        wy[k, 3] = send(half, half, wy_s.at[k, 3], wy_r.at[k, 3], device(x, y + 3, z_hi, z_lo, core))
        to_sibling(k, 3)
        to_sibling(k, 1)

    wc = []

    def to_sibling(k, by):
        slot = wb.at[piece(y + by, z_lo + k, core)]
        wc.append(send(slot, slot, wc_s.at[k, by], wc_r.at[k, by], sibling))

    rows_along_y(0)
    tokens_along_x(0, z_hi)
    to_sibling(0, 0)

    for copy in dz:
        copy.wait_recv()
    block = dts.at[core, y]
    dy = [
        send(block, block, dy_s.at[by], dy_r.at[by], device(x, y + by, z_hi, z_lo, core)) for by in (1, 2, 3)
    ]

    for copy in bz:
        copy.wait_recv()
    for by in (1, 3, 2):
        wz[by - 1].wait_recv()
        rows_along_y(4 - by)
        to_sibling(4 - by, 0)
    relay_along_y(0)
    for copy in dy:
        copy.wait_recv()
    block = dts.at[core]
    dc = send(block, block, dc_s, dc_r, sibling)

    tz[0].wait_recv()
    half = tok.at[x * 4 + (z_hi + 3) % 4, :, pl.ds(0, 2048)]
    tz.append(send(half, half, tz_s.at[2], tz_r.at[2], device(x, y, z_hi + 1, z_lo, core)))
    tz[1].wait_recv()
    half = tok.at[x * 4 + (z_hi + 1) % 4, :, pl.ds(2048, 2048)]
    tz.append(send(half, half, tz_s.at[3], tz_r.at[3], device(x, y, z_hi + 3, z_lo, core)))
    tokens_along_x(1, (z_hi + 3) % 4)
    tokens_along_x(2, (z_hi + 1) % 4)

    for k in (3, 1, 2):
        relay_along_y(k)
    tz[2].wait_recv()
    tz[3].wait_recv()
    tokens_along_x(3, (z_hi + 2) % 4)
    for k in (0, 3, 1, 2):
        wy[k, 2].wait_recv()
        wy[k, 3].wait_recv()
        to_sibling(k, 2)
    for copy in tx:
        copy.wait_recv()
    dc.wait_recv()

    c = lax.axis_index("context")
    t = lax.axis_index("tensor")

    def to_all_contexts(source, slots, ssem, rsem):
        def one(step, carry):
            j = (c + step) % CONTEXTS
            send(source(j), slots.at[c], ssem, rsem, (j, t))
            return carry

        lax.fori_loop(1, CONTEXTS, one, 0)

    def all_of(slots, ssem, rsem):
        several = slots.at[pl.ds(0, CONTEXTS - 1)]
        return pltpu.make_async_remote_copy(
            src_ref=several, dst_ref=several, send_sem=ssem, recv_sem=rsem, device_id=sibling, device_id_type=MESH
        )

    rows = tok[...].reshape(SPAN, 4096)
    dt_cols = jnp.concatenate([dts[p % 2, p // 8, (p // 2) % 4] for p in range(32)], 1)
    dt_raw = lax.dot_general(rows, dt_cols, (((1,), (1,)), ((), ())), preferred_element_type=jnp.float32)
    raw = jnp.concatenate([dt_raw, jnp.zeros((SPAN, 112), jnp.float32)], 1).T[:8]
    head_row = lax.broadcasted_iota(jnp.int32, (8, SPAN), 0)

    def per_head(ref):
        return sum(jnp.where(head_row == h, ref[h], 0.0) for h in range(8))

    raw = raw + per_head(bias_ref)
    steps = jnp.maximum(raw, 0.0) + jnp.log1p(jnp.exp(-jnp.abs(raw)))
    upto = lax.broadcasted_iota(jnp.int32, (SPAN, SPAN), 0) <= lax.broadcasted_iota(jnp.int32, (SPAN, SPAN), 1)
    sums = jnp.dot(
        -per_head(rate_ref) * steps, upto.astype(jnp.float32),
        precision=lax.Precision.HIGHEST, preferred_element_type=jnp.float32,
    )
    last = jnp.broadcast_to(sums[:, SPAN - 1 :], (8, SPAN))
    tails = jnp.exp(last - sums) * steps
    columns = jnp.concatenate([sums, tails, jnp.zeros((112, SPAN), jnp.float32)], 0).T
    low_lanes = lax.broadcasted_iota(jnp.int32, (1, 128), 1) < HEAD_DIM
    whole = jnp.exp(last[:, :128])
    decays[c] = jnp.concatenate(
        [jnp.where(low_lanes, whole[2 * b : 2 * b + 1], whole[2 * b + 1 : 2 * b + 2]) for b in range(4)]
        + [jnp.zeros((4, 128), jnp.float32)],
        0,
    )
    to_all_contexts(lambda j: decays.at[c], decays, decay_s, decay_r)

    def spread(first):
        return jnp.concatenate(
            [
                jnp.where(low_lanes, columns[:, first + 2 * b : first + 2 * b + 1], columns[:, first + 2 * b + 1 : first + 2 * b + 2])
                for b in range(4)
            ],
            1,
        )

    for copy in wc:
        copy.wait_recv()
    both = jnp.dot(rows, wb[...].reshape(4096, 768), preferred_element_type=jnp.float32)
    pre[8:] = both.astype(jnp.bfloat16).astype(jnp.float32)
    rim = send(
        pre.at[pl.ds(SPAN, 8)], pre.at[pl.ds(0, 8)], rim_s, rim_r, ((c + 1) % CONTEXTS, t)
    )
    rim.wait_recv()

    @pl.when(c == 0)
    def _():
        pre[:8] = jnp.zeros((8, 768), jnp.float32)

    def convolved(first, width, taps):
        total = sum(
            taps[k : k + 1].astype(jnp.float32) * pre[5 + k : 5 + k + SPAN, first : first + width] for k in range(CONV)
        )
        return (total / (1.0 + jnp.exp(-total))).astype(jnp.bfloat16)

    b_conv = convolved(512, STATE, conv_bc_ref[group][:, :STATE])
    c_conv = convolved(640, STATE, conv_bc_ref[group][:, STATE:])
    x_conv = convolved(0, 512, conv_x_ref[...])

    weighted = (x_conv.astype(jnp.float32) * spread(8)).astype(jnp.bfloat16)
    state = lax.dot_general(b_conv, weighted, (((0,), (0,)), ((), ())), preferred_element_type=jnp.float32)
    state = state.astype(jnp.bfloat16)
    for j in range(CONTEXTS):
        mine[j] = state[16 * (j // 4) : 16 * (j // 4 + 1), 128 * (j % 4) : 128 * (j % 4 + 1)]
    to_all_contexts(lambda j: mine.at[j], theirs, state_s, state_r)
    theirs[c] = mine[c]

    scores = lax.dot_general(c_conv, b_conv, (((1,), (1,)), ((), ())), preferred_element_type=jnp.float32)
    upto = lax.broadcasted_iota(jnp.int32, (SPAN, SPAN), 0) >= lax.broadcasted_iota(jnp.int32, (SPAN, SPAN), 1)
    scores = jnp.where(upto, scores, 0.0)

    def within(h):
        gaps = jnp.minimum(columns[:, h : h + 1] - sums[h : h + 1], 0.0)
        mixing = (scores * jnp.exp(gaps) * steps[h : h + 1]).astype(jnp.bfloat16)
        here = x_conv[:, h * HEAD_DIM : (h + 1) * HEAD_DIM]
        return (
            jnp.dot(mixing, here, preferred_element_type=jnp.float32) + skip_ref[h] * here.astype(jnp.float32)
        )

    for b in range(4):
        inner[:, 128 * b : 128 * (b + 1)] = jnp.concatenate([within(2 * b), within(2 * b + 1)], 1)

    all_of(decays, decay_s, decay_r).wait_recv()
    all_of(theirs, state_s, state_r).wait_recv()
    carried = jnp.zeros((16, 128), jnp.float32)
    for j in range(CONTEXTS):
        leaving[j] = carried.astype(jnp.bfloat16)
        carried = decays[j, pl.ds(c % 4, 1)] * carried + theirs[j].astype(jnp.float32)
    to_all_contexts(lambda j: leaving.at[j], arriving, start_s, start_r)
    arriving[c] = leaving[c]
    growth = jnp.exp(spread(0))
    all_of(arriving, start_s, start_r).wait_recv()
    start = jnp.concatenate(
        [jnp.concatenate([arriving[4 * i + b] for b in range(4)], 1) for i in range(8)], 0
    )
    mixed = inner[...] + growth * jnp.dot(c_conv, start, preferred_element_type=jnp.float32)
    same_head = (
        lax.broadcasted_iota(jnp.int32, (128, 128), 0) // HEAD_DIM == lax.broadcasted_iota(jnp.int32, (128, 128), 1) // HEAD_DIM
    ).astype(jnp.bfloat16)
    for b in range(4):
        part = mixed[:, 128 * b : 128 * (b + 1)]
        square = part * part
        upper = square.astype(jnp.bfloat16)
        lower = (square - upper.astype(jnp.float32)).astype(jnp.bfloat16)
        total = jnp.dot(upper, same_head, preferred_element_type=jnp.float32) + jnp.dot(
            lower, same_head, preferred_element_type=jnp.float32
        )
        scaled = part * lax.rsqrt(total * (1.0 / HEAD_DIM) + 1e-05) * gain_ref[:, 128 * b : 128 * (b + 1)]
        out_ref[:, 128 * b : 128 * (b + 1)] = scaled.astype(jnp.bfloat16)

    for copy in dz + wz + bz + tz + tx + list(wy.values()) + wc + dy + [dc, rim]:
        copy.wait_send()
    all_of(decays, decay_s, decay_r).wait_send()
    all_of(mine, state_s, state_r).wait_send()
    all_of(leaving, start_s, start_r).wait_send()


def local(
    tokens, x_weight, dt_weight, bc_weight, conv_x, conv_bc, dt_bias, a_rate, d_skip, norm_gain
):
    dma = pltpu.SemaphoreType.DMA
    in_vmem = pl.BlockSpec(memory_space=pltpu.VMEM)
    in_smem = pl.BlockSpec(memory_space=pltpu.SMEM)
    anywhere = pl.BlockSpec(memory_space=pl.ANY)
    return pl.pallas_call(
        layer_kernel,
        out_shape=jax.ShapeDtypeStruct((SPAN, 512), jnp.bfloat16),
        in_specs=[anywhere, anywhere, in_vmem, anywhere, in_vmem, in_vmem, in_smem, in_smem, in_smem, in_vmem],
        out_specs=in_vmem,
        scratch_shapes=[
            pltpu.VMEM((16, 16, 4096), jnp.bfloat16),
            pltpu.VMEM((32, 128, 768), jnp.bfloat16),
            pltpu.VMEM((2, 4, 4, 16, 128), jnp.bfloat16),
            pltpu.VMEM((8 + SPAN, 768), jnp.float32),
            pltpu.VMEM((SPAN, 512), jnp.float32),
            pltpu.VMEM((CONTEXTS, 8, 128), jnp.float32),
            pltpu.VMEM((CONTEXTS, 16, 128), jnp.bfloat16),
            pltpu.VMEM((CONTEXTS, 16, 128), jnp.bfloat16),
            pltpu.VMEM((CONTEXTS, 16, 128), jnp.bfloat16),
            pltpu.VMEM((CONTEXTS, 16, 128), jnp.bfloat16),
            dma((3,)),
            dma((4,)), dma((4,)), dma((4, 4)), dma((4, 4)), dma((4,)), dma((4,)), dma((4,)), dma((4,)),
            dma((4, 4)), dma((4, 4)), dma((4, 4)), dma((4, 4)), dma((4,)), dma((4,)), dma((4,)), dma((4,)), dma, dma,
            dma, dma, dma, dma, dma, dma, dma, dma,
        ],
        compiler_params=pltpu.CompilerParams(collective_id=0, has_side_effects=True, vmem_limit_bytes=50 * 2**20),
        name="layer",
    )(tokens, x_weight, dt_weight, bc_weight, conv_x, conv_bc, dt_bias, a_rate, d_skip, norm_gain.reshape(1, 512))


def solution(mesh):
    in_specs = (
        P(("context", "tensor"), None),
        P("context", "tensor"),
        P("context", "tensor"),
        P(None, "context", None),
        P(None, "tensor"),
        P(),
        P("tensor"),
        P("tensor"),
        P("tensor"),
        P("tensor"),
    )
    out_specs = P("context", "tensor")
    return jax.shard_map(local, mesh=mesh, in_specs=in_specs, out_specs=out_specs, check_vma=False)
```

time: 198 us -> 88.1 us (0.44)
  the two profiles are of different devices: /device:TPU:123 before, /device:TPU:1 now
where the time goes in v2:
time: 88.1 us; the launch traced here: 87.8 us
  Pallas kernels  83.3 us (95%)
  local copies, waits for them, and re-layouts  4.43 us (5%)
    pallas_call x1, Pallas kernels, local(): pl.pallas_call(layer_kernel, out_shape=jax.ShapeDtypeStruct((SPAN, 512),...  83.3 us
    unnamed x20, local copies, waits for them, and re-layouts  4.43 us

profile of v2, /device:TPU:1, one launch (start us, length us, event | category | flops | bytes accessed | tf_op | source)
XLA Modules:
  0.0 87.8 jit_solution(9852674532793121858)
XLA Ops:
  0.0 0.0 copy-start.3
  0.0 0.0 copy-start.4
  0.0 0.0 copy-start.5
  0.0 0.0 copy-start.6
  0.0 0.0 copy-start.7
  0.0 0.0 copy-start.8
  0.0 0.9 copy.11.dt_ref
  0.9 0.0 copy-done.3
  0.9 0.0 copy-done.4
  0.9 0.0 copy-done.5
  0.9 0.0 copy-done.6
  0.9 0.0 copy-done.7
  0.9 0.0 copy-done.8
  0.9 0.0 copy-start
  1.0 1.0 %copy-done = bf16[8,128,256]{2,1,0:T(8,128)(2,1)S(1)} copy-done((bf16[8,128,256]{2,1,0:T(8,128)(2,1)S(1)}, bf16[8,128,256]{2,1,0:T(8,128)(2,1)}, u32[]{:S(2)}) %copy-start) | copy-done | bytes 524312
  2.0 0.0 copy-start.1
  2.0 0.9 %copy-done.1 = bf16[16,4096]{1,0:T(8,128)(2,1)S(1)} copy-done((bf16[16,4096]{1,0:T(8,128)(2,1)S(1)}, bf16[16,4096]{1,0:T(8,128)(2,1)}, u32[]{:S(2)}) %copy-start.1) | copy-done | bytes 131096
  2.9 0.0 copy-start.2
  2.9 0.9 %copy-done.2 = bf16[128,512]{1,0:T(8,128)(2,1)S(1)} copy-done((bf16[128,512]{1,0:T(8,128)(2,1)S(1)}, bf16[128,512]{1,0:T(8,128)(2,1)}, u32[]{:S(2)}) %copy-start.2) | copy-done | bytes 131096
  3.8 83.3 %layer.1 = bf16[256,512]{1,0:T(8,128)(2,1)S(1)} custom-call(bf16[16,4096]{1,0:T(8,128)(2,1)S(1)} %copy-done.1, bf16[128,512]{1,0:T(8,128)(2,1)S(1)} %copy-done.2, bf16[128,8]{1,0:T(8,128)(2,1)S(1)} %copy.11.dt_ref, bf16[8,128,256]{2,1,0:T(8,128)(2,1)S(1)} %copy-done, bf16[4,512]{1,0:T(4,128)(2,1)S(1)} %copy-done.4, bf16[8,4,256]{2,1,0:T(4,128)(2,1)S(1)} %copy-done.3, ...), custom_call_target="tpu_custom_call" | custom-call | tf_op jit(solution)/shard_map/layer/pallas_call | solution.py:327
  87.1 0.7 copy.13
Async XLA Ops:
  0.0 0.9 %copy-start.3 = (bf16[8,4,256]{2,1,0:T(4,128)(2,1)S(1)}, bf16[8,4,256]{2,1,0:T(4,128)(2,1)}, u32[]{:S(2)}) copy-start(bf16[8,4,256]{2,1,0:T(4,128)(2,1)} %conv_bc_ref.1) | copy-start | bytes 49156
  0.0 0.9 %copy-start.4 = (bf16[4,512]{1,0:T(4,128)(2,1)S(1)}, bf16[4,512]{1,0:T(4,128)(2,1)}, u32[]{:S(2)}) copy-start(bf16[4,512]{1,0:T(4,128)(2,1)} %conv_x_ref.1) | copy-start | bytes 12292
  0.0 0.9 %copy-start.5 = (f32[512]{0:T(512)S(1)}, f32[512]{0:T(512)}, u32[]{:S(2)}) copy-start(f32[512]{0:T(512)} %param.19) | copy-start | bytes 6148
  0.0 0.9 %copy-start.6 = (f32[8]{0:T(128)S(1)}, f32[8]{0:T(128)}, u32[]{:S(2)}) copy-start(f32[8]{0:T(128)} %bias_ref.1) | copy-start | bytes 100
  0.0 0.9 %copy-start.7 = (f32[8]{0:T(128)S(1)}, f32[8]{0:T(128)}, u32[]{:S(2)}) copy-start(f32[8]{0:T(128)} %rate_ref.1) | copy-start | bytes 100
  0.0 0.9 %copy-start.8 = (f32[8]{0:T(128)S(1)}, f32[8]{0:T(128)}, u32[]{:S(2)}) copy-start(f32[8]{0:T(128)} %skip_ref.1) | copy-start | bytes 100
  0.9 1.0 %copy-start = (bf16[8,128,256]{2,1,0:T(8,128)(2,1)S(1)}, bf16[8,128,256]{2,1,0:T(8,128)(2,1)}, u32[]{:S(2)}) copy-start(bf16[8,128,256]{2,1,0:T(8,128)(2,1)} %bc_ref.1) | copy-start | bytes 1572868
  2.0 0.9 %copy-start.1 = (bf16[16,4096]{1,0:T(8,128)(2,1)S(1)}, bf16[16,4096]{1,0:T(8,128)(2,1)}, u32[]{:S(2)}) copy-start(bf16[16,4096]{1,0:T(8,128)(2,1)} %tok_ref.1) | copy-start | bytes 393220
  2.9 0.9 %copy-start.2 = (bf16[128,512]{1,0:T(8,128)(2,1)S(1)}, bf16[128,512]{1,0:T(8,128)(2,1)}, u32[]{:S(2)}) copy-start(bf16[128,512]{1,0:T(8,128)(2,1)} %w_ref.1) | copy-start | bytes 393220

commit v3 on v2

--- a/solution.py
+++ b/solution.py
@@ -27,6 +27,17 @@
 def along_z(z, by):
     other = (z + by + 16) % 16
     return other // 4, other % 4
+
+
+ORDER = ((0, 1, 2, 3), (1, 0, 2, 3), (2, 1, 3, 0), (3, 2, 1, 0))
+ONWARD = (None, (1, 1), (-1, -1), (-1, 1))
+
+
+def pick(index, values):
+    out = values[-1]
+    for k in range(len(values) - 2, -1, -1):
+        out = jnp.where(index == k, values[k], out)
+    return out
 
 
 def layer_kernel(
@@ -40,29 +51,38 @@
     x, y, z_hi, z_lo, core = place()
     z = z_hi * 4 + z_lo
     t_own = x * 4 + z_hi
+    c = lax.axis_index("context")
+    t = lax.axis_index("tensor")
     sibling = device(x, y, z_hi, z_lo, 1 - core)
 
-    def send(src, dst, ssem, rsem, dev):
-        copy = pltpu.make_async_remote_copy(
+    def describe(src, dst, ssem, rsem, dev):
+        return pltpu.make_async_remote_copy(
             src_ref=src, dst_ref=dst, send_sem=ssem, recv_sem=rsem, device_id=dev, device_id_type=MESH
         )
+
+    def send(*args):
+        copy = describe(*args)
         copy.start()
         return copy
 
     def piece(y_at, z_at, core_at):
         return (y_at % 4) * 8 + (z_at % 4) * 2 + core_at
+
+    def x_part(ref, p):
+        return ref.at[p, :, pl.ds(0, 512)]
 
     own = piece(y, z_lo, core)
     group = x * 2 + z_hi // 2
     local = [
+        pltpu.make_async_copy(w_ref, x_part(wb, own), local_sem.at[1]),
+        pltpu.make_async_copy(bc_ref.at[group], wb.at[own, :, pl.ds(512, 256)], local_sem.at[2]),
         pltpu.make_async_copy(tok_ref, tok.at[t_own], local_sem.at[0]),
-        pltpu.make_async_copy(w_ref, wb.at[own, :, pl.ds(0, 512)], local_sem.at[1]),
-        pltpu.make_async_copy(bc_ref.at[group], wb.at[own, :, pl.ds(512, 256)], local_sem.at[2]),
     ]
     for copy in local:
         copy.start()
-    square = jnp.concatenate([dt_ref[...].astype(jnp.float32), jnp.zeros((128, 120), jnp.float32)], 1)
-    dts[core, y, z_lo] = square.T[:16].astype(jnp.bfloat16)
+    dts[core, y, z_lo] = jnp.concatenate(
+        [dt_ref[...].astype(jnp.float32), jnp.zeros((8, 128), jnp.float32)], 0
+    ).astype(jnp.bfloat16)
 
     barrier = pltpu.get_barrier_semaphore()
     partners = [device(x, y, z_hi + 1, z_lo, core), device(x, y, z_hi + 3, z_lo, core), sibling]
@@ -72,22 +92,31 @@
         partners.append(device(x, y, z_hi, z_lo + by, core))
     for by in (1, -1, 2, -2):
         partners.append(device(x, y, *along_z(z, by), core))
-    c = lax.axis_index("context")
     for by in (1, CONTEXTS - 1):
-        partners.append(((c + by) % CONTEXTS, t_own))
+        partners.append(((c + by) % CONTEXTS, t))
     for partner in partners:
         pl.semaphore_signal(barrier, inc=1, device_id=partner, device_id_type=MESH)
     pl.semaphore_wait(barrier, len(partners))
 
-    started = []
-    dz = [
-        send(dts.at[core, y, z_lo], dts.at[core, y, z_lo], dz_s.at[by], dz_r.at[by], device(x, y, z_hi, z_lo + by, core))
-        for by in (1, 2, 3)
-    ]
-    wz = [
-        send(w_ref, wb.at[own, :, pl.ds(0, 512)], wz_s.at[by], wz_r.at[by], device(x, y, z_hi, z_lo + by, core))
-        for by in (1, 2, 3)
-    ]
+    arrival = [pick(z_lo, [row[j] for row in ORDER]) for j in range(4)]
+    guarded = []
+
+    def rows_along_z(z_at, onward, sem, condition):
+        to = (z_lo + onward + 4) % 4
+        number = pick(to, [pick(z_at, [row.index(k) for k in range(4)]) for row in ORDER])
+        block = x_part(wb, piece(y, z_at, core))
+        copy = describe(block, block, wz_s.at[sem], wz_r.at[number], device(x, y, z_hi, to, core))
+
+        @pl.when(condition)
+        def _():
+            copy.start()
+
+        guarded.append((condition, copy))
+
+    for copy in local[:2]:
+        copy.wait()
+    rows_along_z(z_lo, 1, 0, z_lo < 3)
+    rows_along_z(z_lo, -1, 1, z_lo > 0)
     bz = []
     for i, (by, first, count) in enumerate(((1, 0, 128), (-1, 0, 128), (2, 0, 64), (-2, 64, 64))):
         hi, lo = along_z(z, by)
@@ -98,92 +127,108 @@
                 bz_s.at[i], bz_r.at[i], device(x, y, hi, lo, core),
             )
         )
-    tz = [
-        send(tok_ref, tok.at[t_own], tz_s.at[0], tz_r.at[0], device(x, y, z_hi + 1, z_lo, core)),
-        send(tok_ref, tok.at[t_own], tz_s.at[1], tz_r.at[1], device(x, y, z_hi + 3, z_lo, core)),
-    ]
-    for copy in local:
-        copy.wait()
+    block = dts.at[core, y, z_lo]
+    dz = [send(block, block, dz_s.at[by], dz_r.at[by], device(x, y, z_hi, z_lo + by, core)) for by in (1, 2, 3)]
+
+    wy = {}
+    wc = {}
+
+    def to_sibling(j, by):
+        slot = wb.at[piece(y + by, arrival[j], core)]
+        wc[j, by] = send(slot, slot, wc_s.at[j, by], wc_r.at[j, by], sibling)
+
+    def rows_along_y(j):
+        slot = wb.at[piece(y, arrival[j], core)]
+        wy[j, 0] = send(slot, slot, wy_s.at[j, 0], wy_r.at[j, 0], device(x, y + 1, z_hi, z_lo, core))
+        wy[j, 1] = send(slot, slot, wy_s.at[j, 1], wy_r.at[j, 1], device(x, y + 3, z_hi, z_lo, core))
+        to_sibling(j, 0)
+
+    def next_rows(j):
+        block = x_part(wb, piece(y, arrival[j], core))
+        describe(block, block, wz_s.at[0], wz_r.at[j], sibling).wait_recv()
+        rows_along_z(arrival[j], jnp.where(z_lo == 1, *ONWARD[j]), 1 + j, (z_lo == 1) | (z_lo == 2))
+        rows_along_y(j)
+
+    def relay_along_y(j):
+        wy[j, 0].wait_recv()
+        half = wb.at[piece(y + 3, arrival[j], core), pl.ds(0, 64)]
+        wy[j, 2] = send(half, half, wy_s.at[j, 2], wy_r.at[j, 2], device(x, y + 1, z_hi, z_lo, core))
+        wy[j, 1].wait_recv()
+        half = wb.at[piece(y + 1, arrival[j], core), pl.ds(64, 64)]
+        wy[j, 3] = send(half, half, wy_s.at[j, 3], wy_r.at[j, 3], device(x, y + 3, z_hi, z_lo, core))
+        to_sibling(j, 3)
+        to_sibling(j, 1)
+
+    def last_along_y(j):
+        wy[j, 2].wait_recv()
+        wy[j, 3].wait_recv()
+        to_sibling(j, 2)
 
     tx = []
-
-    def tokens_along_x(k, hi):
-        slot = tok.at[x * 4 + hi]
-        for by in (1, 2, 3):
-            tx.append(
-                send(slot, slot, tx_s.at[k, by], tx_r.at[k, by], device(x + by, y, z_hi, z_lo, core))
-            )
-
-    wy = {}
-
-    def rows_along_y(k):
-        slot = wb.at[piece(y, z_lo + k, core)]
-        wy[k, 0] = send(slot, slot, wy_s.at[k, 0], wy_r.at[k, 0], device(x, y + 1, z_hi, z_lo, core))
-        wy[k, 1] = send(slot, slot, wy_s.at[k, 1], wy_r.at[k, 1], device(x, y + 3, z_hi, z_lo, core))
-
-    def relay_along_y(k):
-        wy[k, 0].wait_recv()
-        half = wb.at[piece(y + 3, z_lo + k, core), pl.ds(0, 64)]
-        wy[k, 2] = send(half, half, wy_s.at[k, 2], wy_r.at[k, 2], device(x, y + 1, z_hi, z_lo, core))
-        wy[k, 1].wait_recv()
-        half = wb.at[piece(y + 1, z_lo + k, core), pl.ds(64, 64)]
-        wy[k, 3] = send(half, half, wy_s.at[k, 3], wy_r.at[k, 3], device(x, y + 3, z_hi, z_lo, core))
-        to_sibling(k, 3)
-        to_sibling(k, 1)
-
-    wc = []
-
-    def to_sibling(k, by):
-        slot = wb.at[piece(y + by, z_lo + k, core)]
-        wc.append(send(slot, slot, wc_s.at[k, by], wc_r.at[k, by], sibling))
+    tz = {}
+
+    def tokens_along_x(k, hi, columns):
+        slot = tok.at[x * 4 + hi % 4, :, columns]
+        for by in (1, 3, 2):
+            i = len(tx)
+            tx.append(send(slot, slot, tx_s.at[i], tx_r.at[i], device(x + by, y, z_hi, z_lo, core)))
+
+    halves = (pl.ds(0, 2048), pl.ds(2048, 2048))
+    up, down = device(x, y, z_hi + 1, z_lo, core), device(x, y, z_hi + 3, z_lo, core)
+
+    def tokens_along_z():
+        for half in range(2):
+            block = tok.at[t_own, :, halves[half]]
+            tz[0, half] = send(block, block, tz_s.at[0, half], tz_r.at[0, half], up)
+            tz[1, half] = send(block, block, tz_s.at[1, half], tz_r.at[1, half], down)
+
+    def relay_tokens(half):
+        tz[0, half].wait_recv()
+        block = tok.at[x * 4 + (z_hi + 3) % 4, :, pl.ds(half * 2048, 1024)]
+        tz[2, half] = send(block, block, tz_s.at[2, half], tz_r.at[2, half], up)
+        tz[1, half].wait_recv()
+        block = tok.at[x * 4 + (z_hi + 1) % 4, :, pl.ds(half * 2048 + 1024, 1024)]
+        tz[3, half] = send(block, block, tz_s.at[3, half], tz_r.at[3, half], down)
+        tokens_along_x(1, z_hi + 3, halves[half])
+        tokens_along_x(2, z_hi + 1, halves[half])
+
+    def last_tokens(half):
+        tz[2, half].wait_recv()
+        tz[3, half].wait_recv()
+        tokens_along_x(3, z_hi + 2, halves[half])
 
     rows_along_y(0)
-    tokens_along_x(0, z_hi)
-    to_sibling(0, 0)
-
+    local[2].wait()
+    tokens_along_x(0, z_hi, pl.ds(0, 4096))
     for copy in dz:
         copy.wait_recv()
     block = dts.at[core, y]
     dy = [
         send(block, block, dy_s.at[by], dy_r.at[by], device(x, y + by, z_hi, z_lo, core)) for by in (1, 2, 3)
     ]
-
     for copy in bz:
         copy.wait_recv()
-    for by in (1, 3, 2):
-        wz[by - 1].wait_recv()
-        rows_along_y(4 - by)
-        to_sibling(4 - by, 0)
+    next_rows(1)
+    tokens_along_z()
+    next_rows(2)
+    relay_tokens(0)
     relay_along_y(0)
     for copy in dy:
         copy.wait_recv()
     block = dts.at[core]
     dc = send(block, block, dc_s, dc_r, sibling)
-
-    tz[0].wait_recv()
-    half = tok.at[x * 4 + (z_hi + 3) % 4, :, pl.ds(0, 2048)]
-    tz.append(send(half, half, tz_s.at[2], tz_r.at[2], device(x, y, z_hi + 1, z_lo, core)))
-    tz[1].wait_recv()
-    half = tok.at[x * 4 + (z_hi + 1) % 4, :, pl.ds(2048, 2048)]
-    tz.append(send(half, half, tz_s.at[3], tz_r.at[3], device(x, y, z_hi + 3, z_lo, core)))
-    tokens_along_x(1, (z_hi + 3) % 4)
-    tokens_along_x(2, (z_hi + 1) % 4)
-
-    for k in (3, 1, 2):
-        relay_along_y(k)
-    tz[2].wait_recv()
-    tz[3].wait_recv()
-    tokens_along_x(3, (z_hi + 2) % 4)
-    for k in (0, 3, 1, 2):
-        wy[k, 2].wait_recv()
-        wy[k, 3].wait_recv()
-        to_sibling(k, 2)
+    next_rows(3)
+    relay_tokens(1)
+    relay_along_y(1)
+    last_tokens(0)
+    relay_along_y(2)
+    relay_along_y(3)
+    last_tokens(1)
+    for j in range(4):
+        last_along_y(j)
     for copy in tx:
         copy.wait_recv()
     dc.wait_recv()
-
-    c = lax.axis_index("context")
-    t = lax.axis_index("tensor")
 
     def to_all_contexts(source, slots, ssem, rsem):
         def one(step, carry):
@@ -195,9 +240,7 @@
 
     def all_of(slots, ssem, rsem):
         several = slots.at[pl.ds(0, CONTEXTS - 1)]
-        return pltpu.make_async_remote_copy(
-            src_ref=several, dst_ref=several, send_sem=ssem, recv_sem=rsem, device_id=sibling, device_id_type=MESH
-        )
+        return describe(several, several, ssem, rsem, sibling)
 
     rows = tok[...].reshape(SPAN, 4096)
     dt_cols = jnp.concatenate([dts[p % 2, p // 8, (p // 2) % 4] for p in range(32)], 1)
@@ -236,28 +279,41 @@
             1,
         )
 
-    for copy in wc:
-        copy.wait_recv()
-    both = jnp.dot(rows, wb[...].reshape(4096, 768), preferred_element_type=jnp.float32)
+    both = jnp.zeros((SPAN, 768), jnp.float32)
+    for by in (0, 1, 3, 2):
+        for j in range(4):
+            wc[j, by].wait_recv()
+        at = (y + by) % 4
+        some = tok[:, :, pl.ds(pl.multiple_of(at * 1024, 1024), 1024)].reshape(SPAN, 1024)
+        both += jnp.dot(some, wb[pl.ds(at * 8, 8)].reshape(1024, 768), preferred_element_type=jnp.float32)
     pre[8:] = both.astype(jnp.bfloat16).astype(jnp.float32)
     rim = send(
         pre.at[pl.ds(SPAN, 8)], pre.at[pl.ds(0, 8)], rim_s, rim_r, ((c + 1) % CONTEXTS, t)
     )
+    x_taps = conv_x_ref[...].astype(jnp.float32)
+    bc_taps = conv_bc_ref[group].astype(jnp.float32)
+
+    def convolved(first, width, taps, start, count):
+        total = sum(
+            taps[k : k + 1] * pre[start + 5 + k : start + 5 + k + count, first : first + width] for k in range(CONV)
+        )
+        return total / (1.0 + jnp.exp(-total))
+
+    later = (
+        convolved(0, 512, x_taps, 8, SPAN - 8),
+        convolved(512, 256, bc_taps, 8, SPAN - 8),
+    )
     rim.wait_recv()
 
     @pl.when(c == 0)
     def _():
         pre[:8] = jnp.zeros((8, 768), jnp.float32)
 
-    def convolved(first, width, taps):
-        total = sum(
-            taps[k : k + 1].astype(jnp.float32) * pre[5 + k : 5 + k + SPAN, first : first + width] for k in range(CONV)
-        )
-        return (total / (1.0 + jnp.exp(-total))).astype(jnp.bfloat16)
-
-    b_conv = convolved(512, STATE, conv_bc_ref[group][:, :STATE])
-    c_conv = convolved(640, STATE, conv_bc_ref[group][:, STATE:])
-    x_conv = convolved(0, 512, conv_x_ref[...])
+    earlier = (convolved(0, 512, x_taps, 0, 8), convolved(512, 256, bc_taps, 0, 8))
+    x_conv, bc_conv = (
+        jnp.concatenate(pair, 0).astype(jnp.bfloat16) for pair in zip(earlier, later)
+    )
+    b_conv, c_conv = bc_conv[:, :STATE], bc_conv[:, STATE:]
 
     weighted = (x_conv.astype(jnp.float32) * spread(8)).astype(jnp.bfloat16)
     state = lax.dot_general(b_conv, weighted, (((0,), (0,)), ((), ())), preferred_element_type=jnp.float32)
@@ -310,8 +366,14 @@
         scaled = part * lax.rsqrt(total * (1.0 / HEAD_DIM) + 1e-05) * gain_ref[:, 128 * b : 128 * (b + 1)]
         out_ref[:, 128 * b : 128 * (b + 1)] = scaled.astype(jnp.bfloat16)
 
-    for copy in dz + wz + bz + tz + tx + list(wy.values()) + wc + dy + [dc, rim]:
+    for copy in dz + bz + list(tz.values()) + tx + list(wy.values()) + list(wc.values()) + dy + [dc, rim]:
         copy.wait_send()
+    for condition, copy in guarded:
+
+        @pl.when(condition)
+        def _(copy=copy):
+            copy.wait_send()
+
     all_of(decays, decay_s, decay_r).wait_send()
     all_of(mine, state_s, state_r).wait_send()
     all_of(leaving, start_s, start_r).wait_send()
@@ -323,7 +385,7 @@
     dma = pltpu.SemaphoreType.DMA
     in_vmem = pl.BlockSpec(memory_space=pltpu.VMEM)
     in_smem = pl.BlockSpec(memory_space=pltpu.SMEM)
-    anywhere = pl.BlockSpec(memory_space=pl.ANY)
+    anywhere = pl.BlockSpec(memory_space=pltpu.HBM)
     return pl.pallas_call(
         layer_kernel,
         out_shape=jax.ShapeDtypeStruct((SPAN, 512), jnp.bfloat16),
@@ -341,13 +403,13 @@
             pltpu.VMEM((CONTEXTS, 16, 128), jnp.bfloat16),
             pltpu.VMEM((CONTEXTS, 16, 128), jnp.bfloat16),
             dma((3,)),
-            dma((4,)), dma((4,)), dma((4, 4)), dma((4, 4)), dma((4,)), dma((4,)), dma((4,)), dma((4,)),
+            dma((4, 2)), dma((4, 2)), dma((21,)), dma((21,)), dma((5,)), dma((4,)), dma((4,)), dma((4,)),
             dma((4, 4)), dma((4, 4)), dma((4, 4)), dma((4, 4)), dma((4,)), dma((4,)), dma((4,)), dma((4,)), dma, dma,
             dma, dma, dma, dma, dma, dma, dma, dma,
         ],
-        compiler_params=pltpu.CompilerParams(collective_id=0, has_side_effects=True, vmem_limit_bytes=50 * 2**20),
+        compiler_params=pltpu.CompilerParams(collective_id=0, has_side_effects=True, vmem_limit_bytes=60 * 2**20),
         name="layer",
-    )(tokens, x_weight, dt_weight, bc_weight, conv_x, conv_bc, dt_bias, a_rate, d_skip, norm_gain.reshape(1, 512))
+    )(tokens, x_weight, dt_weight.T, bc_weight, conv_x, conv_bc, dt_bias, a_rate, d_skip, norm_gain.reshape(1, 512))
 
 
 def solution(mesh):

time: 88.1 us -> 80.9 us (0.918)
  Pallas kernels: 83.3 us -> 79 us
  local copies, waits for them, and re-layouts: 4.43 us -> 1.67 us
    pallas_call x1, Pallas kernels: 83.3 us -> 79 us  [local(): pl.pallas_call(layer_kernel, out_shape=jax.ShapeDtypeStruct((SPAN, 512),...]
    unnamed x20 -> x1, local copies, waits for them, and re-layouts: 4.43 us -> 1.67 us
where the time goes in v3:
time: 80.9 us; the launch traced here: 80.7 us
  Pallas kernels  79 us (98%)
  local copies, waits for them, and re-layouts  1.67 us (2%)
    pallas_call x1, Pallas kernels, local(): pl.pallas_call(layer_kernel, out_shape=jax.ShapeDtypeStruct((SPAN, 512),...  79 us
    unnamed x1, local copies, waits for them, and re-layouts  1.67 us

profile of v3, /device:TPU:1, one launch (start us, length us, event | category | flops | bytes accessed | tf_op | source)
XLA Modules:
  0.0 80.7 jit_solution(12013567860517499895)
XLA Ops:
  0.0 79.0 %layer.1 = bf16[256,512]{1,0:T(8,128)(2,1)} custom-call(bf16[16,4096]{1,0:T(8,128)(2,1)} %tok_ref.1, bf16[128,512]{1,0:T(8,128)(2,1)} %w_ref.1, bf16[8,128]{1,0:T(8,128)(2,1)} %bitcast.2, bf16[8,128,256]{2,1,0:T(8,128)(2,1)} %bc_ref.1, bf16[4,512]{1,0:T(4,128)(2,1)} %conv_x_ref.1, bf16[8,4,256]{2,1,0:T(4,128)(2,1)} %conv_bc_ref.1, f32[8]{0:T(128)} %bias_ref.1, ...), custom_call_target="tpu_custom_call" | custom-call | tf_op jit(solution)/shard_map/layer/pallas_call | solution.py:389
  79.1 1.7 %copy.12 = bf16[256,512]{1,0:T(8,128)(2,1)} copy(bf16[256,512]{1,0:T(8,128)(2,1)} %layer.1) | data formatting | bytes 524288

commit v4 on v3

--- a/solution.py
+++ b/solution.py
@@ -12,6 +12,8 @@
 SPAN = 256
 CONV = 4
 CONTEXTS = 32
+PARTS = 2
+WIDE = 4096 // PARTS
 
 
 def place():
@@ -43,6 +45,7 @@
 def layer_kernel(
     tok_ref, w_ref, dt_ref, bc_ref, conv_x_ref, conv_bc_ref, bias_ref, rate_ref, skip_ref, gain_ref,
     out_ref,
+    dt_own, x_taps, bc_taps, bias, rate, skip, gain, small_sem,
     tok, wb, dts, pre, inner, decays, mine, theirs, leaving, arriving,
     local_sem, tz_s, tz_r, tx_s, tx_r, wz_s, wz_r, bz_s, bz_r,
     wy_s, wy_r, wc_s, wc_r, dz_s, dz_r, dy_s, dy_r, dc_s, dc_r,
@@ -78,11 +81,17 @@
         pltpu.make_async_copy(bc_ref.at[group], wb.at[own, :, pl.ds(512, 256)], local_sem.at[2]),
         pltpu.make_async_copy(tok_ref, tok.at[t_own], local_sem.at[0]),
     ]
-    for copy in local:
+    small = [
+        pltpu.make_async_copy(src, dst, small_sem.at[i])
+        for i, (src, dst) in enumerate(
+            (
+                (dt_ref, dt_own), (conv_x_ref, x_taps), (conv_bc_ref, bc_taps), (bias_ref, bias),
+                (rate_ref, rate), (skip_ref, skip), (gain_ref, gain),
+            )
+        )
+    ]
+    for copy in local + small:
         copy.start()
-    dts[core, y, z_lo] = jnp.concatenate(
-        [dt_ref[...].astype(jnp.float32), jnp.zeros((8, 128), jnp.float32)], 0
-    ).astype(jnp.bfloat16)
 
     barrier = pltpu.get_barrier_semaphore()
     partners = [device(x, y, z_hi + 1, z_lo, core), device(x, y, z_hi + 3, z_lo, core), sibling]
@@ -127,6 +136,10 @@
                 bz_s.at[i], bz_r.at[i], device(x, y, hi, lo, core),
             )
         )
+    small[0].wait()
+    dts[core, y, z_lo] = jnp.concatenate(
+        [dt_own[...].astype(jnp.float32), jnp.zeros((8, 128), jnp.float32)], 0
+    ).astype(jnp.bfloat16)
     block = dts.at[core, y, z_lo]
     dz = [send(block, block, dz_s.at[by], dz_r.at[by], device(x, y, z_hi, z_lo + by, core)) for by in (1, 2, 3)]
 
@@ -164,42 +177,47 @@
         wy[j, 3].wait_recv()
         to_sibling(j, 2)
 
-    tx = []
+    tx = {}
     tz = {}
 
-    def tokens_along_x(k, hi, columns):
-        slot = tok.at[x * 4 + hi % 4, :, columns]
-        for by in (1, 3, 2):
-            i = len(tx)
-            tx.append(send(slot, slot, tx_s.at[i], tx_r.at[i], device(x + by, y, z_hi, z_lo, core)))
-
-    halves = (pl.ds(0, 2048), pl.ds(2048, 2048))
+    def tokens_along_x(k, hi, part):
+        slot = tok.at[x * 4 + hi % 4, :, columns_of(part)]
+        for i, by in enumerate((1, 3, 2)):
+            tx[k, part, by] = send(
+                slot, slot, tx_s.at[k, part, i], tx_r.at[k, part, i], device(x + by, y, z_hi, z_lo, core)
+            )
+
+    def columns_of(part):
+        return pl.ds(part * WIDE, WIDE)
+
     up, down = device(x, y, z_hi + 1, z_lo, core), device(x, y, z_hi + 3, z_lo, core)
 
     def tokens_along_z():
-        for half in range(2):
-            block = tok.at[t_own, :, halves[half]]
-            tz[0, half] = send(block, block, tz_s.at[0, half], tz_r.at[0, half], up)
-            tz[1, half] = send(block, block, tz_s.at[1, half], tz_r.at[1, half], down)
-
-    def relay_tokens(half):
-        tz[0, half].wait_recv()
-        block = tok.at[x * 4 + (z_hi + 3) % 4, :, pl.ds(half * 2048, 1024)]
-        tz[2, half] = send(block, block, tz_s.at[2, half], tz_r.at[2, half], up)
-        tz[1, half].wait_recv()
-        block = tok.at[x * 4 + (z_hi + 1) % 4, :, pl.ds(half * 2048 + 1024, 1024)]
-        tz[3, half] = send(block, block, tz_s.at[3, half], tz_r.at[3, half], down)
-        tokens_along_x(1, z_hi + 3, halves[half])
-        tokens_along_x(2, z_hi + 1, halves[half])
-
-    def last_tokens(half):
-        tz[2, half].wait_recv()
-        tz[3, half].wait_recv()
-        tokens_along_x(3, z_hi + 2, halves[half])
+        for part in range(PARTS):
+            block = tok.at[t_own, :, columns_of(part)]
+            tz[0, part] = send(block, block, tz_s.at[0, part], tz_r.at[0, part], up)
+            tz[1, part] = send(block, block, tz_s.at[1, part], tz_r.at[1, part], down)
+
+    def relay_tokens(part):
+        tz[0, part].wait_recv()
+        block = tok.at[x * 4 + (z_hi + 3) % 4, :, pl.ds(part * WIDE, WIDE // 2)]
+        tz[2, part] = send(block, block, tz_s.at[2, part], tz_r.at[2, part], up)
+        tz[1, part].wait_recv()
+        block = tok.at[x * 4 + (z_hi + 1) % 4, :, pl.ds(part * WIDE + WIDE // 2, WIDE // 2)]
+        tz[3, part] = send(block, block, tz_s.at[3, part], tz_r.at[3, part], down)
+        tokens_along_x(1, z_hi + 3, part)
+        tokens_along_x(2, z_hi + 1, part)
+
+    def last_tokens(part):
+        tz[2, part].wait_recv()
+        tz[3, part].wait_recv()
+        tokens_along_x(3, z_hi + 2, part)
 
     rows_along_y(0)
     local[2].wait()
-    tokens_along_x(0, z_hi, pl.ds(0, 4096))
+    for part in range(PARTS):
+        tokens_along_x(0, z_hi, part)
+    tokens_along_z()
     for copy in dz:
         copy.wait_recv()
     block = dts.at[core, y]
@@ -209,7 +227,6 @@
     for copy in bz:
         copy.wait_recv()
     next_rows(1)
-    tokens_along_z()
     next_rows(2)
     relay_tokens(0)
     relay_along_y(0)
@@ -226,9 +243,9 @@
     last_tokens(1)
     for j in range(4):
         last_along_y(j)
-    for copy in tx:
+    dc.wait_recv()
+    for copy in wc.values():
         copy.wait_recv()
-    dc.wait_recv()
 
     def to_all_contexts(source, slots, ssem, rsem):
         def one(step, carry):
@@ -242,20 +259,37 @@
         several = slots.at[pl.ds(0, CONTEXTS - 1)]
         return describe(several, several, ssem, rsem, sibling)
 
-    rows = tok[...].reshape(SPAN, 4096)
-    dt_cols = jnp.concatenate([dts[p % 2, p // 8, (p // 2) % 4] for p in range(32)], 1)
-    dt_raw = lax.dot_general(rows, dt_cols, (((1,), (1,)), ((), ())), preferred_element_type=jnp.float32)
+    for copy in small[1:]:
+        copy.wait()
+    both = jnp.zeros((SPAN, 768), jnp.float32)
+    dt_raw = jnp.zeros((SPAN, 16), jnp.float32)
+    count = CONTEXTS // PARTS
+    for part in range(PARTS):
+        for (_, at, _), copy in tx.items():
+            if at == part:
+                copy.wait_recv()
+        some = tok[:, :, part * WIDE : (part + 1) * WIDE].reshape(SPAN, WIDE)
+        pieces = range(part * count, (part + 1) * count)
+        both += jnp.dot(
+            some, wb[part * count : (part + 1) * count].reshape(WIDE, 768), preferred_element_type=jnp.float32
+        )
+        dt_cols = jnp.concatenate([dts[p % 2, p // 8, (p // 2) % 4] for p in pieces], 1)
+        dt_raw += lax.dot_general(some, dt_cols, (((1,), (1,)), ((), ())), preferred_element_type=jnp.float32)
+    pre[8:] = both.astype(jnp.bfloat16).astype(jnp.float32)
+    rim = send(
+        pre.at[pl.ds(SPAN, 8)], pre.at[pl.ds(0, 8)], rim_s, rim_r, ((c + 1) % CONTEXTS, t)
+    )
     raw = jnp.concatenate([dt_raw, jnp.zeros((SPAN, 112), jnp.float32)], 1).T[:8]
-    head_row = lax.broadcasted_iota(jnp.int32, (8, SPAN), 0)
+    diagonal = lax.broadcasted_iota(jnp.int32, (8, 8), 0) == lax.broadcasted_iota(jnp.int32, (8, 8), 1)
 
     def per_head(ref):
-        return sum(jnp.where(head_row == h, ref[h], 0.0) for h in range(8))
-
-    raw = raw + per_head(bias_ref)
+        return jnp.sum(jnp.where(diagonal, jnp.broadcast_to(ref[...], (8, 8)), 0.0), axis=1, keepdims=True)
+
+    raw = raw + per_head(bias)
     steps = jnp.maximum(raw, 0.0) + jnp.log1p(jnp.exp(-jnp.abs(raw)))
     upto = lax.broadcasted_iota(jnp.int32, (SPAN, SPAN), 0) <= lax.broadcasted_iota(jnp.int32, (SPAN, SPAN), 1)
     sums = jnp.dot(
-        -per_head(rate_ref) * steps, upto.astype(jnp.float32),
+        -per_head(rate) * steps, upto.astype(jnp.float32),
         precision=lax.Precision.HIGHEST, preferred_element_type=jnp.float32,
     )
     last = jnp.broadcast_to(sums[:, SPAN - 1 :], (8, SPAN))
@@ -279,19 +313,9 @@
             1,
         )
 
-    both = jnp.zeros((SPAN, 768), jnp.float32)
-    for by in (0, 1, 3, 2):
-        for j in range(4):
-            wc[j, by].wait_recv()
-        at = (y + by) % 4
-        some = tok[:, :, pl.ds(pl.multiple_of(at * 1024, 1024), 1024)].reshape(SPAN, 1024)
-        both += jnp.dot(some, wb[pl.ds(at * 8, 8)].reshape(1024, 768), preferred_element_type=jnp.float32)
-    pre[8:] = both.astype(jnp.bfloat16).astype(jnp.float32)
-    rim = send(
-        pre.at[pl.ds(SPAN, 8)], pre.at[pl.ds(0, 8)], rim_s, rim_r, ((c + 1) % CONTEXTS, t)
-    )
-    x_taps = conv_x_ref[...].astype(jnp.float32)
-    bc_taps = conv_bc_ref[group].astype(jnp.float32)
+
+    x_tap = x_taps[...].astype(jnp.float32)
+    bc_tap = bc_taps[group].astype(jnp.float32)
 
     def convolved(first, width, taps, start, count):
         total = sum(
@@ -300,8 +324,8 @@
         return total / (1.0 + jnp.exp(-total))
 
     later = (
-        convolved(0, 512, x_taps, 8, SPAN - 8),
-        convolved(512, 256, bc_taps, 8, SPAN - 8),
+        convolved(0, 512, x_tap, 8, SPAN - 8),
+        convolved(512, 256, bc_tap, 8, SPAN - 8),
     )
     rim.wait_recv()
 
@@ -309,7 +333,7 @@
     def _():
         pre[:8] = jnp.zeros((8, 768), jnp.float32)
 
-    earlier = (convolved(0, 512, x_taps, 0, 8), convolved(512, 256, bc_taps, 0, 8))
+    earlier = (convolved(0, 512, x_tap, 0, 8), convolved(512, 256, bc_tap, 0, 8))
     x_conv, bc_conv = (
         jnp.concatenate(pair, 0).astype(jnp.bfloat16) for pair in zip(earlier, later)
     )
@@ -332,7 +356,7 @@
         mixing = (scores * jnp.exp(gaps) * steps[h : h + 1]).astype(jnp.bfloat16)
         here = x_conv[:, h * HEAD_DIM : (h + 1) * HEAD_DIM]
         return (
-            jnp.dot(mixing, here, preferred_element_type=jnp.float32) + skip_ref[h] * here.astype(jnp.float32)
+            jnp.dot(mixing, here, preferred_element_type=jnp.float32) + skip[:, h : h + 1] * here.astype(jnp.float32)
         )
 
     for b in range(4):
@@ -363,10 +387,10 @@
         total = jnp.dot(upper, same_head, preferred_element_type=jnp.float32) + jnp.dot(
             lower, same_head, preferred_element_type=jnp.float32
         )
-        scaled = part * lax.rsqrt(total * (1.0 / HEAD_DIM) + 1e-05) * gain_ref[:, 128 * b : 128 * (b + 1)]
+        scaled = part * lax.rsqrt(total * (1.0 / HEAD_DIM) + 1e-05) * gain[:, 128 * b : 128 * (b + 1)]
         out_ref[:, 128 * b : 128 * (b + 1)] = scaled.astype(jnp.bfloat16)
 
-    for copy in dz + bz + list(tz.values()) + tx + list(wy.values()) + list(wc.values()) + dy + [dc, rim]:
+    for copy in dz + bz + list(tz.values()) + list(tx.values()) + list(wy.values()) + list(wc.values()) + dy + [dc, rim]:
         copy.wait_send()
     for condition, copy in guarded:
 
@@ -384,14 +408,21 @@
 ):
     dma = pltpu.SemaphoreType.DMA
     in_vmem = pl.BlockSpec(memory_space=pltpu.VMEM)
-    in_smem = pl.BlockSpec(memory_space=pltpu.SMEM)
     anywhere = pl.BlockSpec(memory_space=pltpu.HBM)
     return pl.pallas_call(
         layer_kernel,
         out_shape=jax.ShapeDtypeStruct((SPAN, 512), jnp.bfloat16),
-        in_specs=[anywhere, anywhere, in_vmem, anywhere, in_vmem, in_vmem, in_smem, in_smem, in_smem, in_vmem],
+        in_specs=[anywhere] * 10,
         out_specs=in_vmem,
         scratch_shapes=[
+            pltpu.VMEM((8, 128), jnp.bfloat16),
+            pltpu.VMEM((4, 512), jnp.bfloat16),
+            pltpu.VMEM((8, 4, 256), jnp.bfloat16),
+            pltpu.VMEM((1, 8), jnp.float32),
+            pltpu.VMEM((1, 8), jnp.float32),
+            pltpu.VMEM((1, 8), jnp.float32),
+            pltpu.VMEM((1, 512), jnp.float32),
+            dma((7,)),
             pltpu.VMEM((16, 16, 4096), jnp.bfloat16),
             pltpu.VMEM((32, 128, 768), jnp.bfloat16),
             pltpu.VMEM((2, 4, 4, 16, 128), jnp.bfloat16),
@@ -403,13 +434,14 @@
             pltpu.VMEM((CONTEXTS, 16, 128), jnp.bfloat16),
             pltpu.VMEM((CONTEXTS, 16, 128), jnp.bfloat16),
             dma((3,)),
-            dma((4, 2)), dma((4, 2)), dma((21,)), dma((21,)), dma((5,)), dma((4,)), dma((4,)), dma((4,)),
+            dma((4, PARTS)), dma((4, PARTS)), dma((4, PARTS, 3)), dma((4, PARTS, 3)), dma((5,)), dma((4,)), dma((4,)), dma((4,)),
             dma((4, 4)), dma((4, 4)), dma((4, 4)), dma((4, 4)), dma((4,)), dma((4,)), dma((4,)), dma((4,)), dma, dma,
             dma, dma, dma, dma, dma, dma, dma, dma,
         ],
         compiler_params=pltpu.CompilerParams(collective_id=0, has_side_effects=True, vmem_limit_bytes=60 * 2**20),
         name="layer",
-    )(tokens, x_weight, dt_weight.T, bc_weight, conv_x, conv_bc, dt_bias, a_rate, d_skip, norm_gain.reshape(1, 512))
+    )(tokens, x_weight, dt_weight.T, bc_weight, conv_x, conv_bc,
+      dt_bias.reshape(1, 8), a_rate.reshape(1, 8), d_skip.reshape(1, 8), norm_gain.reshape(1, 512))
 
 
 def solution(mesh):

time: 80.9 us -> 77.8 us (0.962)
  Pallas kernels: 79 us -> 76 us
    pallas_call x1, Pallas kernels: 79 us -> 76 us  [local(): pl.pallas_call(layer_kernel, out_shape=jax.ShapeDtypeStruct((SPAN, 512),...]
where the time goes in v4:
time: 77.8 us; the launch traced here: 77.7 us
  Pallas kernels  76 us (98%)
  local copies, waits for them, and re-layouts  1.67 us (2%)
    pallas_call x1, Pallas kernels, local(): pl.pallas_call(layer_kernel, out_shape=jax.ShapeDtypeStruct((SPAN, 512),...  76 us
    unnamed x1, local copies, waits for them, and re-layouts  1.67 us

profile of v4, /device:TPU:1, one launch (start us, length us, event | category | flops | bytes accessed | tf_op | source)
XLA Modules:
  0.0 77.7 jit_solution(2467104930642916917)
XLA Ops:
  0.0 76.0 %layer.1 = bf16[256,512]{1,0:T(8,128)(2,1)} custom-call(bf16[16,4096]{1,0:T(8,128)(2,1)} %tok_ref.1, bf16[128,512]{1,0:T(8,128)(2,1)} %w_ref.1, bf16[8,128]{1,0:T(8,128)(2,1)} %bitcast.5, bf16[8,128,256]{2,1,0:T(8,128)(2,1)} %bc_ref.1, bf16[4,512]{1,0:T(4,128)(2,1)} %conv_x_ref.1, bf16[8,4,256]{2,1,0:T(4,128)(2,1)} %conv_bc_ref.1, f32[1,8]{1,0:T(1,128)} %bitcast.7, ...), custom_call_target="tpu_custom_call" | custom-call | tf_op jit(solution)/shard_map/layer/pallas_call | solution.py:412
  76.0 1.7 %copy.12 = bf16[256,512]{1,0:T(8,128)(2,1)} copy(bf16[256,512]{1,0:T(8,128)(2,1)} %layer.1) | data formatting | bytes 524288

commit v5 on v4

--- a/solution.py
+++ b/solution.py
@@ -12,6 +12,7 @@
 SPAN = 256
 CONV = 4
 CONTEXTS = 32
+OWNERS = 16
 PARTS = 2
 WIDE = 4096 // PARTS
 
@@ -180,8 +181,8 @@
     tx = {}
     tz = {}
 
-    def tokens_along_x(k, hi, part):
-        slot = tok.at[x * 4 + hi % 4, :, columns_of(part)]
+    def tokens_along_x(k, hi, part, columns=None):
+        slot = tok.at[x * 4 + hi % 4, :, columns_of(part) if columns is None else columns]
         for i, by in enumerate((1, 3, 2)):
             tx[k, part, by] = send(
                 slot, slot, tx_s.at[k, part, i], tx_r.at[k, part, i], device(x + by, y, z_hi, z_lo, core)
@@ -215,8 +216,7 @@
 
     rows_along_y(0)
     local[2].wait()
-    for part in range(PARTS):
-        tokens_along_x(0, z_hi, part)
+    tokens_along_x(0, z_hi, 0, pl.ds(0, 4096))
     tokens_along_z()
     for copy in dz:
         copy.wait_recv()
@@ -224,9 +224,17 @@
     dy = [
         send(block, block, dy_s.at[by], dy_r.at[by], device(x, y + by, z_hi, z_lo, core)) for by in (1, 2, 3)
     ]
-    for copy in bz:
+    nearer = jnp.where(z_lo == 0, 1, 0)
+
+    def neighbour_rows(which):
+        slot = wb.at[own, :, pl.ds(512, 256)]
+        describe(slot, slot, bz_s.at[0], bz_r.at[which], sibling).wait_recv()
+
+    neighbour_rows(nearer)
+    next_rows(1)
+    neighbour_rows(1 - nearer)
+    for copy in bz[2:]:
         copy.wait_recv()
-    next_rows(1)
     next_rows(2)
     relay_tokens(0)
     relay_along_y(0)
@@ -247,17 +255,27 @@
     for copy in wc.values():
         copy.wait_recv()
 
-    def to_all_contexts(source, slots, ssem, rsem):
+    owner = (z_lo == 1) | (z_lo == 2)
+    nearest = y * 4 + (z_lo // 2) * 2 + core
+
+    def context_of(o):
+        return (o // 4) * 8 + (1 + (o // 2) % 2) * 2 + o % 2
+
+    def to_owners(source, slots, ssem, rsem):
         def one(step, carry):
-            j = (c + step) % CONTEXTS
-            send(source(j), slots.at[c], ssem, rsem, (j, t))
+            o = (nearest + step) % OWNERS
+            send(source(o), slots.at[c], ssem, rsem, (context_of(o), t))
             return carry
 
-        lax.fori_loop(1, CONTEXTS, one, 0)
-
-    def all_of(slots, ssem, rsem):
-        several = slots.at[pl.ds(0, CONTEXTS - 1)]
-        return describe(several, several, ssem, rsem, sibling)
+        @pl.when(~owner)
+        def _():
+            one(0, 0)
+
+        lax.fori_loop(1, OWNERS, one, 0)
+
+    def several(slots, count, ssem, rsem):
+        some = slots.at[pl.ds(0, count)]
+        return describe(some, some, ssem, rsem, sibling)
 
     for copy in small[1:]:
         copy.wait()
@@ -302,7 +320,7 @@
         + [jnp.zeros((4, 128), jnp.float32)],
         0,
     )
-    to_all_contexts(lambda j: decays.at[c], decays, decay_s, decay_r)
+    to_owners(lambda o: decays.at[c], decays, decay_s, decay_r)
 
     def spread(first):
         return jnp.concatenate(
@@ -342,10 +360,12 @@
     weighted = (x_conv.astype(jnp.float32) * spread(8)).astype(jnp.bfloat16)
     state = lax.dot_general(b_conv, weighted, (((0,), (0,)), ((), ())), preferred_element_type=jnp.float32)
     state = state.astype(jnp.bfloat16)
-    for j in range(CONTEXTS):
-        mine[j] = state[16 * (j // 4) : 16 * (j // 4 + 1), 128 * (j % 4) : 128 * (j % 4 + 1)]
-    to_all_contexts(lambda j: mine.at[j], theirs, state_s, state_r)
-    theirs[c] = mine[c]
+    for o in range(OWNERS):
+        for k in range(2):
+            b = 2 * (o % 2) + k
+            mine[o, k] = state[16 * (o // 2) : 16 * (o // 2 + 1), 128 * b : 128 * (b + 1)]
+    to_owners(lambda o: mine.at[o], theirs, state_s, state_r)
+    theirs[c] = mine[nearest]
 
     scores = lax.dot_general(c_conv, b_conv, (((1,), (1,)), ((), ())), preferred_element_type=jnp.float32)
     upto = lax.broadcasted_iota(jnp.int32, (SPAN, SPAN), 0) >= lax.broadcasted_iota(jnp.int32, (SPAN, SPAN), 1)
@@ -362,18 +382,36 @@
     for b in range(4):
         inner[:, 128 * b : 128 * (b + 1)] = jnp.concatenate([within(2 * b), within(2 * b + 1)], 1)
 
-    all_of(decays, decay_s, decay_r).wait_recv()
-    all_of(theirs, state_s, state_r).wait_recv()
-    carried = jnp.zeros((16, 128), jnp.float32)
-    for j in range(CONTEXTS):
-        leaving[j] = carried.astype(jnp.bfloat16)
-        carried = decays[j, pl.ds(c % 4, 1)] * carried + theirs[j].astype(jnp.float32)
-    to_all_contexts(lambda j: leaving.at[j], arriving, start_s, start_r)
-    arriving[c] = leaving[c]
+    @pl.when(owner)
+    def _():
+        several(decays, CONTEXTS - 1, decay_s, decay_r).wait_recv()
+        several(theirs, CONTEXTS - 1, state_s, state_r).wait_recv()
+        carried = jnp.zeros((2, 16, 128), jnp.float32)
+        for j in range(CONTEXTS):
+            leaving[j] = carried.astype(jnp.bfloat16)
+            decay = decays[j, pl.ds(2 * core, 2)].reshape(2, 1, 128)
+            carried = decay * carried + theirs[j].astype(jnp.float32)
+
+        def one(step, carry):
+            j = (c + step) % CONTEXTS
+            send(leaving.at[j], arriving.at[nearest], start_s, start_r, (j, t))
+            return carry
+
+        lax.fori_loop(1, CONTEXTS, one, 0)
+        arriving[nearest] = leaving[c]
+
     growth = jnp.exp(spread(0))
-    all_of(arriving, start_s, start_r).wait_recv()
+
+    @pl.when(owner)
+    def _():
+        several(arriving, OWNERS - 1, start_s, start_r).wait_recv()
+
+    @pl.when(~owner)
+    def _():
+        several(arriving, OWNERS, start_s, start_r).wait_recv()
+
     start = jnp.concatenate(
-        [jnp.concatenate([arriving[4 * i + b] for b in range(4)], 1) for i in range(8)], 0
+        [jnp.concatenate([arriving[2 * i + b // 2, b % 2] for b in range(4)], 1) for i in range(8)], 0
     )
     mixed = inner[...] + growth * jnp.dot(c_conv, start, preferred_element_type=jnp.float32)
     same_head = (
@@ -398,9 +436,17 @@
         def _(copy=copy):
             copy.wait_send()
 
-    all_of(decays, decay_s, decay_r).wait_send()
-    all_of(mine, state_s, state_r).wait_send()
-    all_of(leaving, start_s, start_r).wait_send()
+
+    @pl.when(owner)
+    def _():
+        several(decays, OWNERS - 1, decay_s, decay_r).wait_send()
+        several(mine, OWNERS - 1, state_s, state_r).wait_send()
+        several(leaving, CONTEXTS - 1, start_s, start_r).wait_send()
+
+    @pl.when(~owner)
+    def _():
+        several(decays, OWNERS, decay_s, decay_r).wait_send()
+        several(mine, OWNERS, state_s, state_r).wait_send()
 
 
 def local(
@@ -429,10 +475,10 @@
             pltpu.VMEM((8 + SPAN, 768), jnp.float32),
             pltpu.VMEM((SPAN, 512), jnp.float32),
             pltpu.VMEM((CONTEXTS, 8, 128), jnp.float32),
-            pltpu.VMEM((CONTEXTS, 16, 128), jnp.bfloat16),
-            pltpu.VMEM((CONTEXTS, 16, 128), jnp.bfloat16),
-            pltpu.VMEM((CONTEXTS, 16, 128), jnp.bfloat16),
-            pltpu.VMEM((CONTEXTS, 16, 128), jnp.bfloat16),
+            pltpu.VMEM((OWNERS, 2, 16, 128), jnp.bfloat16),
+            pltpu.VMEM((CONTEXTS, 2, 16, 128), jnp.bfloat16),
+            pltpu.VMEM((CONTEXTS, 2, 16, 128), jnp.bfloat16),
+            pltpu.VMEM((OWNERS, 2, 16, 128), jnp.bfloat16),
             dma((3,)),
             dma((4, PARTS)), dma((4, PARTS)), dma((4, PARTS, 3)), dma((4, PARTS, 3)), dma((5,)), dma((4,)), dma((4,)), dma((4,)),
             dma((4, 4)), dma((4, 4)), dma((4, 4)), dma((4, 4)), dma((4,)), dma((4,)), dma((4,)), dma((4,)), dma, dma,

time: 77.8 us -> 77.4 us (level)
  no operation moved by 1% of the time
where the time goes in v5:
time: 77.4 us; the launch traced here: 77.3 us
  Pallas kernels  75.6 us (98%)
  local copies, waits for them, and re-layouts  1.67 us (2%)
    pallas_call x1, Pallas kernels, local(): pl.pallas_call(layer_kernel, out_shape=jax.ShapeDtypeStruct((SPAN, 512),...  75.6 us
    unnamed x1, local copies, waits for them, and re-layouts  1.67 us

profile of v5, /device:TPU:1, one launch (start us, length us, event | category | flops | bytes accessed | tf_op | source)
XLA Modules:
  0.0 77.3 jit_solution(7239963452253475570)
XLA Ops:
  0.0 75.6 %layer.1 = bf16[256,512]{1,0:T(8,128)(2,1)} custom-call(bf16[16,4096]{1,0:T(8,128)(2,1)} %tok_ref.1, bf16[128,512]{1,0:T(8,128)(2,1)} %w_ref.1, bf16[8,128]{1,0:T(8,128)(2,1)} %bitcast.5, bf16[8,128,256]{2,1,0:T(8,128)(2,1)} %bc_ref.1, bf16[4,512]{1,0:T(4,128)(2,1)} %conv_x_ref.1, bf16[8,4,256]{2,1,0:T(4,128)(2,1)} %conv_bc_ref.1, f32[1,8]{1,0:T(1,128)} %bitcast.7, ...), custom_call_target="tpu_custom_call" | custom-call | tf_op jit(solution)/shard_map/layer/pallas_call | solution.py:458
  75.6 1.7 %copy.12 = bf16[256,512]{1,0:T(8,128)(2,1)} copy(bf16[256,512]{1,0:T(8,128)(2,1)} %layer.1) | data formatting | bytes 524288

commit v6 on v5

--- a/solution.py
+++ b/solution.py
@@ -46,7 +46,7 @@
 def layer_kernel(
     tok_ref, w_ref, dt_ref, bc_ref, conv_x_ref, conv_bc_ref, bias_ref, rate_ref, skip_ref, gain_ref,
     out_ref,
-    dt_own, x_taps, bc_taps, bias, rate, skip, gain, small_sem,
+    bias, rate, skip, gain, small_sem,
     tok, wb, dts, pre, inner, decays, mine, theirs, leaving, arriving,
     local_sem, tz_s, tz_r, tx_s, tx_r, wz_s, wz_r, bz_s, bz_r,
     wy_s, wy_r, wc_s, wc_r, dz_s, dz_r, dy_s, dy_r, dc_s, dc_r,
@@ -86,8 +86,7 @@
         pltpu.make_async_copy(src, dst, small_sem.at[i])
         for i, (src, dst) in enumerate(
             (
-                (dt_ref, dt_own), (conv_x_ref, x_taps), (conv_bc_ref, bc_taps), (bias_ref, bias),
-                (rate_ref, rate), (skip_ref, skip), (gain_ref, gain),
+                (bias_ref, bias), (rate_ref, rate), (skip_ref, skip), (gain_ref, gain),
             )
         )
     ]
@@ -137,9 +136,8 @@
                 bz_s.at[i], bz_r.at[i], device(x, y, hi, lo, core),
             )
         )
-    small[0].wait()
     dts[core, y, z_lo] = jnp.concatenate(
-        [dt_own[...].astype(jnp.float32), jnp.zeros((8, 128), jnp.float32)], 0
+        [dt_ref[...].astype(jnp.float32), jnp.zeros((8, 128), jnp.float32)], 0
     ).astype(jnp.bfloat16)
     block = dts.at[core, y, z_lo]
     dz = [send(block, block, dz_s.at[by], dz_r.at[by], device(x, y, z_hi, z_lo + by, core)) for by in (1, 2, 3)]
@@ -277,7 +275,7 @@
         some = slots.at[pl.ds(0, count)]
         return describe(some, some, ssem, rsem, sibling)
 
-    for copy in small[1:]:
+    for copy in small:
         copy.wait()
     both = jnp.zeros((SPAN, 768), jnp.float32)
     dt_raw = jnp.zeros((SPAN, 16), jnp.float32)
@@ -332,8 +330,8 @@
         )
 
 
-    x_tap = x_taps[...].astype(jnp.float32)
-    bc_tap = bc_taps[group].astype(jnp.float32)
+    x_tap = conv_x_ref[...].astype(jnp.float32)
+    bc_tap = conv_bc_ref[group].astype(jnp.float32)
 
     def convolved(first, width, taps, start, count):
         total = sum(
@@ -458,17 +456,14 @@
     return pl.pallas_call(
         layer_kernel,
         out_shape=jax.ShapeDtypeStruct((SPAN, 512), jnp.bfloat16),
-        in_specs=[anywhere] * 10,
+        in_specs=[anywhere, anywhere, in_vmem, anywhere, in_vmem, in_vmem] + [anywhere] * 4,
         out_specs=in_vmem,
         scratch_shapes=[
-            pltpu.VMEM((8, 128), jnp.bfloat16),
-            pltpu.VMEM((4, 512), jnp.bfloat16),
-            pltpu.VMEM((8, 4, 256), jnp.bfloat16),
             pltpu.VMEM((1, 8), jnp.float32),
             pltpu.VMEM((1, 8), jnp.float32),
             pltpu.VMEM((1, 8), jnp.float32),
             pltpu.VMEM((1, 512), jnp.float32),
-            dma((7,)),
+            dma((4,)),
             pltpu.VMEM((16, 16, 4096), jnp.bfloat16),
             pltpu.VMEM((32, 128, 768), jnp.bfloat16),
             pltpu.VMEM((2, 4, 4, 16, 128), jnp.bfloat16),

time: 77.4 us -> 78 us (level)
  no operation moved by 1% of the time
where the time goes in v6:
time: 78 us; the launch traced here: 77.8 us
  Pallas kernels  76.1 us (98%)
  local copies, waits for them, and re-layouts  1.67 us (2%)
    pallas_call x1, Pallas kernels, local(): pl.pallas_call(layer_kernel, out_shape=jax.ShapeDtypeStruct((SPAN, 512),...  76.1 us
    unnamed x1, local copies, waits for them, and re-layouts  1.67 us

profile of v6, /device:TPU:1, one launch (start us, length us, event | category | flops | bytes accessed | tf_op | source)
XLA Modules:
  0.0 77.8 jit_solution(17654634583543918509)
XLA Ops:
  0.0 76.1 %layer.1 = bf16[256,512]{1,0:T(8,128)(2,1)} custom-call(bf16[16,4096]{1,0:T(8,128)(2,1)} %tok_ref.1, bf16[128,512]{1,0:T(8,128)(2,1)} %w_ref.1, bf16[8,128]{1,0:T(8,128)(2,1)} %bitcast.5, bf16[8,128,256]{2,1,0:T(8,128)(2,1)} %bc_ref.1, bf16[4,512]{1,0:T(4,128)(2,1)} %conv_x_ref.1, bf16[8,4,256]{2,1,0:T(4,128)(2,1)} %conv_bc_ref.1, f32[1,8]{1,0:T(1,128)} %bitcast.7, ...), custom_call_target="tpu_custom_call" | custom-call | tf_op jit(solution)/shard_map/layer/pallas_call | solution.py:456
  76.2 1.7 %copy.12 = bf16[256,512]{1,0:T(8,128)(2,1)} copy(bf16[256,512]{1,0:T(8,128)(2,1)} %layer.1) | data formatting | bytes 524288
